TPU v7x, 256 devices: a whole 4x4x8 slice. The times are simulated.
256 devices in a mesh: rows: 32 (over z_lo, y, x), cols: 8 (over z_hi, core).
Axes of the slice: x: 4, y: 4, z: 8 (z_hi: 4, z_lo: 2; z = z_hi * 2 + z_lo), core: 2. Of those that a mesh axis runs over, the one named last changes fastest.
Arguments:
- offsets: int32 [32, 131072], P('cols', 'rows'), may hold values from -1024 to 1024
- weights: float32 [32, 131072], P('cols', 'rows'), may hold values from 0.004 to 0.06
- seeds: float32 [64, 131072], P(None, ('rows', 'cols')), may hold values from -6 to 6
Outputs:
- scores: float32 [64, 131072], P(None, ('rows', 'cols'))
All inputs are finite; a program needn't handle non-finite values.
Results may differ from a plain program's by a relative error of at most 0.00007.
Values sent between devices are 32-bit elements; how exact they have to be, the bound alone decides.
No kernel may reach another device: no remote copies, remote signals or barrier semaphores. Data moves between devices by JAX's collectives and lax.ppermute only.
A program may use at most 64 MiB of HBM per device.

v0:
```python
import math

import jax
import jax.numpy as jnp
from jax import lax
from jax.sharding import PartitionSpec as P

BLK = 256
HB = 4
ITERS = 3


def with_halo(cells, sides, width):
    for axis, dim in sides:
        count = lax.axis_size(axis)
        ends = count - 1
        head = lax.slice_in_dim(cells, 0, width, axis=dim)
        tail = lax.slice_in_dim(cells, cells.shape[dim] - width, cells.shape[dim], axis=dim)
        cells = jnp.concatenate(
            [
                lax.ppermute(tail, axis, [(i, (i + 1) % count) for i in range(ends)]),
                cells,
                lax.ppermute(head, axis, [((i + 1) % count, i) for i in range(ends)]),
            ],
            axis=dim,
        )
    return cells


def neighbour_sum(padded, offsets, weights, width):
    slots, events = offsets.shape
    block = math.gcd(events, 128)
    span = block + 2 * width
    group = math.gcd(slots, 4)
    rounds = slots // group
    lanes = jnp.arange(block, dtype=jnp.int32)
    column_ids = jnp.arange(span, dtype=jnp.int32)

    def one_block(number):
        begin = number * block
        local_places = lax.dynamic_slice_in_dim(offsets, begin, block, 1) + lanes[None, :] + width
        local_weights = lax.dynamic_slice_in_dim(weights, begin, block, 1)

        def add_group(turn, matrix):
            hits = local_places[:, None, :] == column_ids[None, :, None]
            return matrix + jnp.sum(jnp.where(hits, local_weights[:, None, :], 0.0), axis=0)

        matrix = lax.fori_loop(0, rounds, add_group, jnp.zeros((span, block), jnp.float32))
        window = lax.dynamic_slice_in_dim(padded, begin, span, 1)
        return jnp.dot(
            window, matrix, precision=lax.Precision.HIGHEST, preferred_element_type=jnp.float32
        )

    numbers = jnp.arange(events // block, dtype=jnp.int32)
    pieces = lax.map(one_block, numbers)
    return jnp.moveaxis(pieces, 0, 1).reshape(padded.shape[0], events)


def on_device(offsets, weights, seeds):
    width = HB * BLK
    scores = seeds
    for step in range(ITERS):
        panel = lax.all_gather(scores, "cols", axis=1, tiled=True)
        padded = with_halo(panel, (("rows", 1),), width)
        mine = lax.psum_scatter(
            neighbour_sum(padded, offsets, weights, width), "cols", scatter_dimension=1, tiled=True
        )
        scores = 0.9 * mine + 0.1 * seeds
    return scores


def solution(mesh):
    in_specs = (P("cols", "rows"), P("cols", "rows"), P(None, ("rows", "cols")))
    out_specs = P(None, ("rows", "cols"))
    return jax.shard_map(
        on_device, mesh=mesh, in_specs=in_specs, out_specs=out_specs, check_vma=False
    )
```

profile of v0, /device:TPU:33, one launch (start us, length us, event | category | flops | bytes accessed | tf_op | source)
XLA Modules:
  0.0 727.0 jit_solution(13190886978986764788)
XLA Ops:
  7.3 33.8 %all-gather.4.cloned.1.call-done = f32[64,4096]{1,0:T(8,128)} async-done(((f32[64,512]{1,0:T(8,128)}), f32[64,4096]{1,0:T(8,128)}) %all-gather.4.cloned.1.call-update) | async-done | bytes 1048592 | tf_op jit(solution)/shard_map/all_gather | solution.py:63
  42.2 3.5 collective-permute-start
  45.7 6.0 collective-permute-start.1
  51.7 4.2 collective-permute-done
  58.1 147.7 %while.33 = (s32[]{:T(128)}, f32[32,64,128]{2,1,0:T(8,128)}, s32[32]{0:T(128)S(1)}, f32[64,6144]{1,0:T(8,128)S(1)}, s32[4,4096]{1,0:T(4,128)}, /*index=5*/f32[4,...) while((s32[]{:T(128)}, f32[32,64,128]{2,1,0:T(8,128)}, ...), condition=%wide.region_2.0_spmd.clone, body=%wide.region_0.2_spmd.clone.sunk | while | flops 216974336 | bytes 2831052 | solution.py:55
  84.3 1.4 fusion.48
  144.3 1.4 fusion.48
  162.8 1.4 fusion.48
  205.8 2.3 copy_bitcast_fusion.2
  208.2 37.8 %reduce-scatter.4.cloned.1.call-done = f32[64,512]{1,0:T(8,128)} async-done(((f32[64,4096]{1,0:T(8,128)}), f32[64,512]{1,0:T(8,128)}) %reduce-scatter.4.cloned.1.call-update) | async-done | bytes 131088 | tf_op jit(solution)/shard_map/reduce_scatter | solution.py:65
  245.9 1.6 multiply_add_fusion.2
  247.6 30.0 %all-gather.6.cloned.1.call-done = f32[64,4096]{1,0:T(8,128)} async-done(((f32[64,512]{1,0:T(8,128)}), f32[64,4096]{1,0:T(8,128)}) %all-gather.6.cloned.1.call-update) | async-done | bytes 1048592 | tf_op jit(solution)/shard_map/all_gather | solution.py:63
  278.8 3.5 collective-permute-start.2
  282.3 6.0 collective-permute-start.3
  288.3 4.2 collective-permute-done.2
  294.6 147.7 %while.34 = (s32[]{:T(128)}, f32[32,64,128]{2,1,0:T(8,128)}, s32[32]{0:T(128)S(1)}, f32[64,6144]{1,0:T(8,128)S(1)}, s32[4,4096]{1,0:T(4,128)}, /*index=5*/f32[4,...) while((s32[]{:T(128)}, f32[32,64,128]{2,1,0:T(8,128)}, ...), condition=%wide.region_6.7_spmd.clone, body=%wide.region_4.6_spmd.clone.sunk | while | flops 216974336 | bytes 2831052 | solution.py:55
  320.9 1.4 fusion.52
  380.9 1.4 fusion.52
  399.4 1.4 fusion.52
  442.4 2.3 copy_bitcast_fusion.1
  444.7 37.8 %reduce-scatter.6.cloned.1.call-done = f32[64,512]{1,0:T(8,128)} async-done(((f32[64,4096]{1,0:T(8,128)}), f32[64,512]{1,0:T(8,128)}) %reduce-scatter.6.cloned.1.call-update) | async-done | bytes 131088 | tf_op jit(solution)/shard_map/reduce_scatter | solution.py:65
  482.5 1.6 multiply_add_fusion.1
  484.1 29.6 %all-gather.8.cloned.1.call-done = f32[64,4096]{1,0:T(8,128)} async-done(((f32[64,512]{1,0:T(8,128)}), f32[64,4096]{1,0:T(8,128)}) %all-gather.8.cloned.1.call-update) | async-done | bytes 1048592 | tf_op jit(solution)/shard_map/all_gather | solution.py:63
  514.9 3.5 collective-permute-start.4
  518.4 6.0 collective-permute-start.5
  524.4 4.2 collective-permute-done.4
  530.8 147.7 %while.35 = (s32[]{:T(128)}, f32[32,64,128]{2,1,0:T(8,128)}, s32[32]{0:T(128)S(1)}, f32[64,6144]{1,0:T(8,128)S(1)}, s32[4,4096]{1,0:T(4,128)}, /*index=5*/f32[4,...) while((s32[]{:T(128)}, f32[32,64,128]{2,1,0:T(8,128)}, ...), condition=%wide.region_10.11_spmd.clone, body=%wide.region_8.0_spmd.clone.sunk | while | flops 216974336 | bytes 2831052 | solution.py:55
  630.9 1.4 fusion.56
  635.5 1.4 fusion.56
  678.5 2.3 copy_bitcast_fusion
  680.8 37.8 %reduce-scatter.8.cloned.1.call-done = f32[64,512]{1,0:T(8,128)} async-done(((f32[64,4096]{1,0:T(8,128)}), f32[64,512]{1,0:T(8,128)}) %reduce-scatter.8.cloned.1.call-update) | async-done | bytes 131088 | tf_op jit(solution)/shard_map/reduce_scatter | solution.py:65
  718.6 1.6 multiply_add_fusion
  (507 shorter events, 378.7 us)
Async XLA Ops:
  6.5 34.5 %all-gather.4.cloned.1.call-start = ((), (), s32[]{:S(2)}) async-start(), calls=%async_computation.3 | async-start | bytes 1179648 | tf_op jit(solution)/shard_map/all_gather | solution.py:63
  7.3 238.7 %reduce-scatter.4.cloned.1.call-start = ((), (), s32[]{:S(2)}) async-start(), calls=%async_computation.4 | async-start | bytes 1179648 | tf_op jit(solution)/shard_map/reduce_scatter | solution.py:65
  41.1 15.8 %copy-start.2 = (f32[64,4096]{1,0:T(8,128)S(1)}, f32[64,4096]{1,0:T(8,128)}, u32[]{:S(2)}) copy-start(f32[64,4096]{1,0:T(8,128)} %all-gather.4.cloned.1.call-done) | copy-start | bytes 3145732
  42.2 13.7 %collective-permute-start = (f32[64,1024]{1,0:T(8,128)S(1)}, f32[64,1024]{1,0:T(8,128)S(1)}, u32[]{:S(2)}, u32[]{:S(2)}) collective-permute-start(f32[64,1024]{1,0:T(8,128)S(1)} %get-tuple-element.264), channel_id=1, source_target_pairs={{0,8},{8,16},{16,24},{24,32},{32,40},{40,48},{48,56},{56,64},{64,7... | collective-permute-start | bytes 786440 | tf_op jit(solution)/shard_map/ppermute | solution.py:21
  45.7 11.1 %collective-permute-start.1 = (f32[64,1024]{1,0:T(8,128)S(1)}, f32[64,1024]{1,0:T(8,128)S(1)}, u32[]{:S(2)}, u32[]{:S(2)}) collective-permute-start(f32[64,1024]{1,0:T(8,128)S(1)} %get-tuple-element.265), channel_id=1, source_target_pairs={{8,0},{16,8},{24,16},{32,24},{40,32},{48,40},{56,48},{64,56},{72,6... | collective-permute-start | bytes 786440 | tf_op jit(solution)/shard_map/ppermute | solution.py:23
  205.8 40.1 %copy-start.3 = (f32[64,512]{1,0:T(8,128)S(1)}, f32[64,512]{1,0:T(8,128)}, u32[]{:S(2)}) copy-start(f32[64,512]{1,0:T(8,128)} %param.11) | copy-start | bytes 393220
  208.1 69.5 %all-gather.6.cloned.1.call-start = ((), (), s32[]{:S(2)}) async-start(), calls=%async_computation.5 | async-start | bytes 1179648 | tf_op jit(solution)/shard_map/all_gather | solution.py:63
  247.5 234.9 %reduce-scatter.6.cloned.1.call-start = ((), (), s32[]{:S(2)}) async-start(), calls=%async_computation.6 | async-start | bytes 1179648 | tf_op jit(solution)/shard_map/reduce_scatter | solution.py:65
  277.6 15.8 %copy-start = (f32[64,4096]{1,0:T(8,128)S(1)}, f32[64,4096]{1,0:T(8,128)}, u32[]{:S(2)}) copy-start(f32[64,4096]{1,0:T(8,128)} %all-gather.6.cloned.1.call-done) | copy-start | bytes 3145732
  278.8 13.7 %collective-permute-start.2 = (f32[64,1024]{1,0:T(8,128)S(1)}, f32[64,1024]{1,0:T(8,128)S(1)}, u32[]{:S(2)}, u32[]{:S(2)}) collective-permute-start(f32[64,1024]{1,0:T(8,128)S(1)} %get-tuple-element.262), channel_id=1, source_target_pairs={{0,8},{8,16},{16,24},{24,32},{32,40},{40,48},{48,56},{56,64},{64,7... | collective-permute-start | bytes 786440 | tf_op jit(solution)/shard_map/ppermute | solution.py:21
  282.3 11.1 %collective-permute-start.3 = (f32[64,1024]{1,0:T(8,128)S(1)}, f32[64,1024]{1,0:T(8,128)S(1)}, u32[]{:S(2)}, u32[]{:S(2)}) collective-permute-start(f32[64,1024]{1,0:T(8,128)S(1)} %get-tuple-element.263), channel_id=1, source_target_pairs={{8,0},{16,8},{24,16},{32,24},{40,32},{48,40},{56,48},{64,56},{72,6... | collective-permute-start | bytes 786440 | tf_op jit(solution)/shard_map/ppermute | solution.py:23
  444.7 69.1 %all-gather.8.cloned.1.call-start = ((), (), s32[]{:S(2)}) async-start(), calls=%async_computation.7 | async-start | bytes 1179648 | tf_op jit(solution)/shard_map/all_gather | solution.py:63
  484.1 234.5 %reduce-scatter.8.cloned.1.call-start = ((), (), s32[]{:S(2)}) async-start(), calls=%async_computation.8 | async-start | bytes 1179648 | tf_op jit(solution)/shard_map/reduce_scatter | solution.py:65
  513.8 15.8 %copy-start.1 = (f32[64,4096]{1,0:T(8,128)S(1)}, f32[64,4096]{1,0:T(8,128)}, u32[]{:S(2)}) copy-start(f32[64,4096]{1,0:T(8,128)} %all-gather.8.cloned.1.call-done) | copy-start | bytes 3145732
  514.9 13.7 %collective-permute-start.4 = (f32[64,1024]{1,0:T(8,128)S(1)}, f32[64,1024]{1,0:T(8,128)S(1)}, u32[]{:S(2)}, u32[]{:S(2)}) collective-permute-start(f32[64,1024]{1,0:T(8,128)S(1)} %get-tuple-element.260), channel_id=1, source_target_pairs={{0,8},{8,16},{16,24},{24,32},{32,40},{40,48},{48,56},{56,64},{64,7... | collective-permute-start | bytes 786440 | tf_op jit(solution)/shard_map/ppermute | solution.py:21
  518.4 11.1 %collective-permute-start.5 = (f32[64,1024]{1,0:T(8,128)S(1)}, f32[64,1024]{1,0:T(8,128)S(1)}, u32[]{:S(2)}, u32[]{:S(2)}) collective-permute-start(f32[64,1024]{1,0:T(8,128)S(1)} %get-tuple-element.261), channel_id=1, source_target_pairs={{8,0},{16,8},{24,16},{32,24},{40,32},{48,40},{56,48},{64,56},{72,6... | collective-permute-start | bytes 786440 | tf_op jit(solution)/shard_map/ppermute | solution.py:23
Sparse Core Ops, SparseCore 0:
  9.2 31.8 all-gather.3
  208.2 37.6 reduce-scatter.3
  247.8 29.8 all-gather.5
  444.8 37.6 reduce-scatter.5
  484.2 29.5 all-gather.7
  680.9 37.6 reduce-scatter.7
where the time goes:
time: 736 us; the launch traced here: 727 us
  waiting for transfers between devices  223 us (30%)
  local copies, waits for them, and re-layouts  138 us (19%)
  matrix products  137 us (19%)
  other arithmetic  123 us (17%)
  loops' own time  63.7 us (9%)
  starting transfers between devices  28.7 us (4%)
  between operations  13.6 us (2%)
    dot_general x96, matrix products, one_block(): jnp.dot(window, matrix, precision=lax.Precision.HIGHEST, preferred_elemen...  137 us
    reduce_scatter x3, waiting for transfers between devices, on_device(): lax.psum_scatter(neighbour_sum(padded, offsets, weights, width), 'cols',...  113 us
    all_gather x3, waiting for transfers between devices, on_device(): panel = lax.all_gather(scores, 'cols', axis=1, tiled=True)  93.4 us
    dynamic_slice x96, local copies, waits for them, and re-layouts, one_block(): local_weights = lax.dynamic_slice_in_dim(weights, begin, block, 1)  66 us
    add x96, other arithmetic, one_block(): lax.dynamic_slice_in_dim(offsets, begin, block, 1) + lanes[None, :] + width  65.8 us
    another operation x3, loops' own time, neighbour_sum(): pieces = lax.map(one_block, numbers)  63.7 us
    dynamic_slice x96, local copies, waits for them, and re-layouts, neighbour_sum(): pieces = lax.map(one_block, numbers)  58 us
    reduce_sum x96, other arithmetic, add_group(): jnp.sum(jnp.where(hits, local_weights[:, None, :], 0.0), axis=0)  52.6 us
  transfers between devices with their start and end apart: 12, of which 12 were waited for; matrix products, arithmetic and copies ran while one was open for 0% of the time, Pallas kernels for 0%

commit v1 on v0

v1 whole, which is shorter than its diff:
```python
import functools

import jax
import jax.numpy as jnp
from jax import lax
from jax.experimental import pallas as pl
from jax.experimental.pallas import tpu as pltpu
from jax.sharding import PartitionSpec as P

HW = 1024
ITERS = 3
LANES = 128
BLOCK = 256
TILES = (BLOCK + 2 * HW) // LANES
SPAN = TILES * LANES
AXES = ("rows", "cols")
NT = (((1,), (1,)), ((), ()))


def build_kernel(edges_ref, high_ref, low_ref, tile_ref, lane_ref, whigh_ref, wlow_ref):
    events = edges_ref.shape[1]
    lane = lax.broadcasted_iota(jnp.int32, (LANES, LANES), 1)
    row = lax.broadcasted_iota(jnp.int32, (LANES, LANES), 0)
    is_offset = (lane & 4) == 0
    for part in range(events // LANES):
        rows = slice(part * LANES, (part + 1) * LANES)
        cells = edges_ref[:, rows]
        turned = jnp.concatenate([cells, cells], axis=0).T
        offset = jnp.where(is_offset, turned, pltpu.roll(turned, 4, 1)).astype(jnp.int32)
        weight = jnp.where(is_offset, pltpu.roll(turned, LANES - 4, 1), turned)
        place = offset + row + (HW + part * LANES % BLOCK)
        tile_ref[rows] = (place >> 7).astype(jnp.float32)
        lane_ref[rows] = (place & (LANES - 1)).astype(jnp.float32)
        high = weight.astype(jnp.bfloat16).astype(jnp.float32)
        whigh_ref[rows] = high
        wlow_ref[rows] = weight - high

    sub = lax.broadcasted_iota(jnp.int32, (8, LANES), 0)
    lane8 = lax.broadcasted_iota(jnp.int32, (8, LANES), 1)
    owner = (lane8 >> 6) * 2 + ((lane8 >> 2) & 1)
    masks = [sub == owner, sub == owner + 4]
    lane_ids = lax.broadcasted_iota(jnp.int32, (LANES, LANES), 0).astype(jnp.float32).astype(jnp.bfloat16)
    two = lax.broadcasted_iota(jnp.int32, (16, LANES), 0)
    two = (two >> 3).astype(jnp.float32).astype(jnp.bfloat16)
    one = jnp.ones((), jnp.bfloat16)
    zero = jnp.zeros((), jnp.bfloat16)

    def eight(at):
        tile, lanes, whigh, wlow = (ref[pl.ds(at, 8), :] for ref in (tile_ref, lane_ref, whigh_ref, wlow_ref))
        twice = lambda x: jnp.concatenate([x, x], axis=0).astype(jnp.bfloat16)
        wh, wl = twice(whigh), twice(wlow)
        left, right = [], []
        highs, lows = [], []
        for mask in masks:
            mine = twice(jnp.where(mask, tile, -1.0)) - two
            hits = [mine == jnp.asarray(2.0 * step, jnp.bfloat16) for step in range(TILES // 2)]
            highs.append(jnp.concatenate([jnp.where(hit, wh, zero) for hit in hits], axis=0))
            lows.append(jnp.concatenate([jnp.where(hit, wl, zero) for hit in hits], axis=0))
            spot = jnp.sum(jnp.where(mask, lanes, 0.0), axis=0, keepdims=True)
            spot = jnp.broadcast_to(spot, (LANES, LANES)).astype(jnp.bfloat16)
            right.append(jnp.where(spot == lane_ids, one, zero))
        left = jnp.concatenate(highs + lows, axis=1)
        right = jnp.concatenate(right + right, axis=1)
        return lax.dot_general(left, right, NT, preferred_element_type=jnp.float32)

    def sixteen(turn, _):
        at = pl.multiple_of(turn * 16, 16)
        first, second = eight(at), eight(at + 8)
        for step in range(TILES):
            both = jnp.concatenate([first[step * 8:step * 8 + 8], second[step * 8:step * 8 + 8]], axis=0)
            high = both.astype(jnp.bfloat16)
            columns = slice(step * LANES, (step + 1) * LANES)
            high_ref[pl.ds(at, 16), columns] = high
            low_ref[pl.ds(at, 16), columns] = (both - high.astype(jnp.float32)).astype(jnp.bfloat16)
        return 0

    lax.fori_loop(0, events // 16, sixteen, 0)


def build(edges):
    events = edges.shape[1]
    out = jax.ShapeDtypeStruct((events, SPAN), jnp.bfloat16)
    return pl.pallas_call(
        build_kernel,
        out_shape=(out, out),
        scratch_shapes=[pltpu.VMEM((events, LANES), jnp.float32)] * 4,
        compiler_params=pltpu.CompilerParams(vmem_limit_bytes=32 * 2**20),
        name="build",
    )(edges)


def apply_kernel(high_ref, low_ref, seeds_ref, *refs):
    *panel_refs, out_ref, window_ref = refs
    channels, events = out_ref.shape
    for number, ref in enumerate(panel_refs):
        value = ref[...]
        high = value.astype(jnp.bfloat16)
        columns = slice(number * events, (number + 1) * events)
        window_ref[:channels, columns] = high
        window_ref[channels:, columns] = (value - high.astype(jnp.float32)).astype(jnp.bfloat16)
    for part in range(events // BLOCK):
        rows = slice(part * BLOCK, (part + 1) * BLOCK)
        window = window_ref[:, part * BLOCK:part * BLOCK + SPAN]
        both = lax.dot_general(window, high_ref[rows], NT, preferred_element_type=jnp.float32)
        rest = lax.dot_general(window[:channels], low_ref[rows], NT, preferred_element_type=jnp.float32)
        total = both[:channels] + (both[channels:] + rest)
        out_ref[:, rows] = 0.9 * total + 0.1 * seeds_ref[:, rows]


def apply(matrix, seeds, panels):
    channels, events = seeds.shape
    return pl.pallas_call(
        apply_kernel,
        out_shape=jax.ShapeDtypeStruct(seeds.shape, jnp.float32),
        scratch_shapes=[pltpu.VMEM((2 * channels, len(panels) * events), jnp.bfloat16)],
        compiler_params=pltpu.CompilerParams(vmem_limit_bytes=32 * 2**20),
        name="apply",
    )(*matrix, seeds, *panels)


def shifted(cells, step, count):
    pairs = [(i, i + step) for i in range(count) if 0 <= i + step < count]
    return lax.ppermute(cells, AXES, pairs)


def on_device(offsets, weights, seeds, *, count):
    reach = HW // seeds.shape[1]
    edges = jnp.concatenate([offsets.astype(jnp.float32), weights], axis=0)
    edges = lax.all_to_all(edges, "cols", split_axis=1, concat_axis=0, tiled=True)
    matrix = build(edges)
    scores = seeds
    for _ in range(ITERS):
        before = [shifted(scores, step, count) for step in range(reach, 0, -1)]
        after = [shifted(scores, -step, count) for step in range(1, reach + 1)]
        scores = apply(matrix, seeds, [*before, scores, *after])
    return scores


def solution(mesh):
    count = mesh.shape["rows"] * mesh.shape["cols"]
    in_specs = (P("cols", "rows"), P("cols", "rows"), P(None, AXES))
    return jax.shard_map(
        functools.partial(on_device, count=count),
        mesh=mesh, in_specs=in_specs, out_specs=P(None, AXES), check_vma=False,
    )
```

time: 736 us -> 98.3 us (0.13); the launches traced: 727 us -> 97.8 us
  waiting for transfers between devices: 223 us -> 24.7 us
  local copies, waits for them, and re-layouts: 138 us -> 0.91 us
  matrix products: 137 us -> 0 us
  other arithmetic: 123 us -> 2.38 us
  loops' own time: 63.7 us -> 0 us
  starting transfers between devices: 28.7 us -> 55.8 us
  Pallas kernels: 0 us -> 13.8 us
  between operations: 13.6 us -> 0.19 us
    dot_general x96 -> x0, matrix products: 137 us -> none  [one_block(): jnp.dot(window, matrix, precision=lax.Precision.HIGHEST, preferred_elemen...]
    dynamic_slice x192 -> x0, local copies, waits for them, and re-layouts: 124 us -> none  [the longest x96 66 us: one_block(): local_weights = lax.dynamic_slice_in_dim(weights, begin, block, 1)]
    reduce_scatter x3 -> x0, waiting for transfers between devices: 113 us -> none  [on_device(): lax.psum_scatter(neighbour_sum(padded, offsets, weights, width), 'cols',...]
    all_gather x3 -> x0, waiting for transfers between devices: 93.4 us -> none  [on_device(): panel = lax.all_gather(scores, 'cols', axis=1, tiled=True)]
    add x99 -> x0, other arithmetic: 70.6 us -> none  [the longest x96 65.8 us: one_block(): lax.dynamic_slice_in_dim(offsets, begin, block, 1) + lanes[None, :] + width]
    another operation x3 -> x0, loops' own time: 63.7 us -> none  [neighbour_sum(): pieces = lax.map(one_block, numbers)]
    reduce_sum x96 -> x0, other arithmetic: 52.6 us -> none  [add_group(): jnp.sum(jnp.where(hits, local_weights[:, None, :], 0.0), axis=0)]
    ppermute x6 -> x12, starting transfers between devices: 28.5 us -> 47.5 us  [shifted(): return lax.ppermute(cells, AXES, pairs)]
  transfers between devices with their start and end apart: 12 -> 13, of which waited for: 12 -> 3; matrix products, arithmetic and copies ran while one was open for 0% -> 0% of each run, Pallas kernels for 0% -> 9%
where the time goes in v1:
time: 98.3 us; the launch traced here: 97.8 us
  starting transfers between devices  55.8 us (57%)
  waiting for transfers between devices  24.7 us (25%)
  Pallas kernels  13.8 us (14%)
  other arithmetic  2.38 us (2%)
    ppermute x12, starting transfers between devices, shifted(): return lax.ppermute(cells, AXES, pairs)  47.5 us
    ppermute x12, waiting for transfers between devices, shifted(): return lax.ppermute(cells, AXES, pairs)  24.7 us
    pallas_call x1, Pallas kernels, build(): pl.pallas_call(build_kernel, out_shape=(out, out), scratch_shapes=[pltpu....  8.38 us
    all_to_all x1, starting transfers between devices, on_device(): lax.all_to_all(edges, 'cols', split_axis=1, concat_axis=0, tiled=True)  8.24 us
    pallas_call x3, Pallas kernels, apply(): pl.pallas_call(apply_kernel, out_shape=jax.ShapeDtypeStruct(seeds.shape,...  5.45 us
  transfers between devices with their start and end apart: 13, of which 3 were waited for; matrix products, arithmetic and copies ran while one was open for 0% of the time, Pallas kernels for 9%

profile of v1, /device:TPU:33, one launch (start us, length us, event | category | flops | bytes accessed | tf_op | source)
XLA Modules:
  0.0 97.8 jit_solution(8845423079383509538)
XLA Ops:
  0.0 0.9 convert_element_type.3
  0.9 1.5 %pad_maximum_fusion = f32[8,4096]{1,0:T(8,128)} fusion(f32[4,4096]{1,0:T(4,128)} %param.4, f32[4,4096]{1,0:T(4,128)S(1)} %convert_element_type.3), kind=kLoop, calls=%fused_computation | loop fusion | flops 32768 | bytes 262144 | tf_op jit(solution)/shard_map/concatenate | solution.py:128
  2.4 8.2 %all-to-all-start = ((f32[8,8,512]{2,0,1:T(8,128)}), f32[8,8,512]{2,0,1:T(8,128)S(1)}, u32[]{:S(2)}, u32[]{:S(2)}) async-start(f32[8,8,512]{2,0,1:T(8,128)} %bitcast), calls=%async_computation | async-start | bytes 262144 | tf_op jit(solution)/shard_map/all_to_all | solution.py:129
  10.6 10.5 %collective-permute-start.3 = (f32[64,512]{1,0:T(8,128)}, f32[64,512]{1,0:T(8,128)S(1)}, u32[]{:S(2)}, u32[]{:S(2)}) collective-permute-start(f32[64,512]{1,0:T(8,128)} %seeds_ref.5), channel_id=1, source_target_pairs={{2,0},{3,1},{4,2},{5,3},{6,4},{7,5},{8,6},{9,7},{10,8},{11,9},{12,... | collective-permute-start | bytes 393224 | tf_op jit(solution)/shard_map/ppermute | solution.py:123
  21.1 2.6 %collective-permute-start.2 = (f32[64,512]{1,0:T(8,128)}, f32[64,512]{1,0:T(8,128)S(1)}, u32[]{:S(2)}, u32[]{:S(2)}) collective-permute-start(f32[64,512]{1,0:T(8,128)} %seeds_ref.5), channel_id=1, source_target_pairs={{1,0},{2,1},{3,2},{4,3},{5,4},{6,5},{7,6},{8,7},{9,8},{10,9},{11,1... | collective-permute-start | bytes 393224 | tf_op jit(solution)/shard_map/ppermute | solution.py:123
  23.7 3.9 %collective-permute-start.1 = (f32[64,512]{1,0:T(8,128)}, f32[64,512]{1,0:T(8,128)S(1)}, u32[]{:S(2)}, u32[]{:S(2)}) collective-permute-start(f32[64,512]{1,0:T(8,128)} %seeds_ref.5), channel_id=1, source_target_pairs={{0,1},{1,2},{2,3},{3,4},{4,5},{5,6},{6,7},{7,8},{8,9},{9,10},{10,1... | collective-permute-start | bytes 393224 | tf_op jit(solution)/shard_map/ppermute | solution.py:123
  27.6 1.9 %collective-permute-start = (f32[64,512]{1,0:T(8,128)}, f32[64,512]{1,0:T(8,128)S(1)}, u32[]{:S(2)}, u32[]{:S(2)}) collective-permute-start(f32[64,512]{1,0:T(8,128)} %seeds_ref.5), channel_id=1, source_target_pairs={{0,2},{1,3},{2,4},{3,5},{4,6},{5,7},{6,8},{7,9},{8,10},{9,11},{10,... | collective-permute-start | bytes 393224 | tf_op jit(solution)/shard_map/ppermute | solution.py:123
  29.5 0.0 all-to-all-done
  29.5 8.4 %build.1 = (bf16[512,2304]{1,0:T(8,128)(2,1)S(1)}, bf16[512,2304]{1,0:T(8,128)(2,1)S(1)}) custom-call(f32[64,512]{1,0:T(8,128)S(1)} %bitcast.4), custom_call_target="tpu_custom_call" | custom-call | tf_op jit(solution)/shard_map/build/pallas_call | solution.py:83
  37.9 0.0 collective-permute-done.3.refs_4_
  37.9 0.0 collective-permute-done.2.refs_3_
  37.9 0.0 collective-permute-done.1.refs_1_
  37.9 4.2 %collective-permute-done.refs_0_ = f32[64,512]{1,0:T(8,128)S(1)} collective-permute-done((f32[64,512]{1,0:T(8,128)}, f32[64,512]{1,0:T(8,128)S(1)}, u32[]{:S(2)}, u32[]{:S(2)}) %collective-permute-start) | collective-permute-done | bytes 131104 | tf_op jit(solution)/shard_map/ppermute | solution.py:123
  42.1 0.9 copy-done
  43.0 1.6 %apply.3.refs_2_ = f32[64,512]{1,0:T(8,128)S(1)} custom-call(bf16[512,2304]{1,0:T(8,128)(2,1)S(1)} %get-tuple-element.7.high_ref, bf16[512,2304]{1,0:T(8,128)(2,1)S(1)} %get-tuple-element.8.low_ref, f32[64,512]{1,0:T(8,128)S(1)} %copy-done, f32[64,512]{1,0:T(8,128)S(1)} %collective-permute-done.refs_0_, f32[64,512]{1,0:T(8,128)S(1)} %collective-permute-done.1.refs_1_, ...), custom_call_target="tpu_custom_call" | custom-call | tf_op jit(solution)/shard_map/apply/pallas_call | solution.py:112
  44.6 6.4 %collective-permute-start.7 = (f32[64,512]{1,0:T(8,128)S(1)}, f32[64,512]{1,0:T(8,128)S(1)}, u32[]{:S(2)}, u32[]{:S(2)}) collective-permute-start(f32[64,512]{1,0:T(8,128)S(1)} %apply.3.refs_2_), channel_id=1, source_target_pairs={{2,0},{3,1},{4,2},{5,3},{6,4},{7,5},{8,6},{9,7},{10,8},{11,9},{12,... | collective-permute-start | bytes 393224 | tf_op jit(solution)/shard_map/ppermute | solution.py:123
  51.1 2.3 %collective-permute-start.6 = (f32[64,512]{1,0:T(8,128)S(1)}, f32[64,512]{1,0:T(8,128)S(1)}, u32[]{:S(2)}, u32[]{:S(2)}) collective-permute-start(f32[64,512]{1,0:T(8,128)S(1)} %apply.3.refs_2_), channel_id=1, source_target_pairs={{1,0},{2,1},{3,2},{4,3},{5,4},{6,5},{7,6},{8,7},{9,8},{10,9},{11,1... | collective-permute-start | bytes 393224 | tf_op jit(solution)/shard_map/ppermute | solution.py:123
  53.4 4.1 %collective-permute-start.5 = (f32[64,512]{1,0:T(8,128)S(1)}, f32[64,512]{1,0:T(8,128)S(1)}, u32[]{:S(2)}, u32[]{:S(2)}) collective-permute-start(f32[64,512]{1,0:T(8,128)S(1)} %apply.3.refs_2_), channel_id=1, source_target_pairs={{0,1},{1,2},{2,3},{3,4},{4,5},{5,6},{6,7},{7,8},{8,9},{9,10},{10,1... | collective-permute-start | bytes 393224 | tf_op jit(solution)/shard_map/ppermute | solution.py:123
  57.5 1.9 %collective-permute-start.4 = (f32[64,512]{1,0:T(8,128)S(1)}, f32[64,512]{1,0:T(8,128)S(1)}, u32[]{:S(2)}, u32[]{:S(2)}) collective-permute-start(f32[64,512]{1,0:T(8,128)S(1)} %apply.3.refs_2_), channel_id=1, source_target_pairs={{0,2},{1,3},{2,4},{3,5},{4,6},{5,7},{6,8},{7,9},{8,10},{9,11},{10,... | collective-permute-start | bytes 393224 | tf_op jit(solution)/shard_map/ppermute | solution.py:123
  59.5 0.0 collective-permute-done.7.refs_4_
  59.5 0.0 collective-permute-done.6.refs_3_
  59.5 0.0 collective-permute-done.5.refs_1_
  59.5 12.4 %collective-permute-done.4.refs_0_ = f32[64,512]{1,0:T(8,128)S(1)} collective-permute-done((f32[64,512]{1,0:T(8,128)S(1)}, f32[64,512]{1,0:T(8,128)S(1)}, u32[]{:S(2)}, u32[]{:S(2)}) %collective-permute-start.4) | collective-permute-done | bytes 131104 | tf_op jit(solution)/shard_map/ppermute | solution.py:123
  71.9 1.6 %apply.4.refs_2_ = f32[64,512]{1,0:T(8,128)S(1)} custom-call(bf16[512,2304]{1,0:T(8,128)(2,1)S(1)} %get-tuple-element.7.high_ref, bf16[512,2304]{1,0:T(8,128)(2,1)S(1)} %get-tuple-element.8.low_ref, f32[64,512]{1,0:T(8,128)S(1)} %copy-done.1, f32[64,512]{1,0:T(8,128)S(1)} %collective-permute-done.4.refs_0_, f32[64,512]{1,0:T(8,128)S(1)} %collective-permute-done.5.refs_1_, ...), custom_call_target="tpu_custom_call" | custom-call | tf_op jit(solution)/shard_map/apply/pallas_call | solution.py:112
  73.5 2.6 %collective-permute-start.11 = (f32[64,512]{1,0:T(8,128)S(1)}, f32[64,512]{1,0:T(8,128)S(1)}, u32[]{:S(2)}, u32[]{:S(2)}) collective-permute-start(f32[64,512]{1,0:T(8,128)S(1)} %apply.4.refs_2_), channel_id=1, source_target_pairs={{2,0},{3,1},{4,2},{5,3},{6,4},{7,5},{8,6},{9,7},{10,8},{11,9},{12,... | collective-permute-start | bytes 393224 | tf_op jit(solution)/shard_map/ppermute | solution.py:123
  76.1 1.9 %collective-permute-start.10 = (f32[64,512]{1,0:T(8,128)S(1)}, f32[64,512]{1,0:T(8,128)S(1)}, u32[]{:S(2)}, u32[]{:S(2)}) collective-permute-start(f32[64,512]{1,0:T(8,128)S(1)} %apply.4.refs_2_), channel_id=1, source_target_pairs={{1,0},{2,1},{3,2},{4,3},{5,4},{6,5},{7,6},{8,7},{9,8},{10,9},{11,1... | collective-permute-start | bytes 393224 | tf_op jit(solution)/shard_map/ppermute | solution.py:123
  78.0 4.5 %collective-permute-start.9 = (f32[64,512]{1,0:T(8,128)S(1)}, f32[64,512]{1,0:T(8,128)S(1)}, u32[]{:S(2)}, u32[]{:S(2)}) collective-permute-start(f32[64,512]{1,0:T(8,128)S(1)} %apply.4.refs_2_), channel_id=1, source_target_pairs={{0,1},{1,2},{2,3},{3,4},{4,5},{5,6},{6,7},{7,8},{8,9},{9,10},{10,1... | collective-permute-start | bytes 393224 | tf_op jit(solution)/shard_map/ppermute | solution.py:123
  82.6 4.8 %collective-permute-start.8 = (f32[64,512]{1,0:T(8,128)S(1)}, f32[64,512]{1,0:T(8,128)S(1)}, u32[]{:S(2)}, u32[]{:S(2)}) collective-permute-start(f32[64,512]{1,0:T(8,128)S(1)} %apply.4.refs_2_), channel_id=1, source_target_pairs={{0,2},{1,3},{2,4},{3,5},{4,6},{5,7},{6,8},{7,9},{8,10},{9,11},{10,... | collective-permute-start | bytes 393224 | tf_op jit(solution)/shard_map/ppermute | solution.py:123
  87.4 0.0 collective-permute-done.11.refs_4_
  87.4 0.0 collective-permute-done.9.refs_1_
  87.4 8.1 %collective-permute-done.8.refs_0_ = f32[64,512]{1,0:T(8,128)S(1)} collective-permute-done((f32[64,512]{1,0:T(8,128)S(1)}, f32[64,512]{1,0:T(8,128)S(1)}, u32[]{:S(2)}, u32[]{:S(2)}) %collective-permute-start.8) | collective-permute-done | bytes 131104 | tf_op jit(solution)/shard_map/ppermute | solution.py:123
  95.5 2.3 %apply.5 = f32[64,512]{1,0:T(8,128)} custom-call(bf16[512,2304]{1,0:T(8,128)(2,1)S(1)} %get-tuple-element.7.high_ref, bf16[512,2304]{1,0:T(8,128)(2,1)S(1)} %get-tuple-element.8.low_ref, f32[64,512]{1,0:T(8,128)S(1)} %copy-done.1, f32[64,512]{1,0:T(8,128)S(1)} %collective-permute-done.8.refs_0_, f32[64,512]{1,0:T(8,128)S(1)} %collective-permute-done.9.refs_1_, ...), custom_call_target="tpu_custom_call" | custom-call | tf_op jit(solution)/shard_map/apply/pallas_call | solution.py:112
  (4 shorter events, 0.0 us)
Async XLA Ops:
  2.4 27.1 %all-to-all-start = ((f32[8,8,512]{2,0,1:T(8,128)}), f32[8,8,512]{2,0,1:T(8,128)S(1)}, u32[]{:S(2)}, u32[]{:S(2)}) async-start(f32[8,8,512]{2,0,1:T(8,128)} %bitcast), calls=%async_computation | async-start | bytes 262144 | tf_op jit(solution)/shard_map/all_to_all | solution.py:129
  10.6 27.3 %collective-permute-start.3 = (f32[64,512]{1,0:T(8,128)}, f32[64,512]{1,0:T(8,128)S(1)}, u32[]{:S(2)}, u32[]{:S(2)}) collective-permute-start(f32[64,512]{1,0:T(8,128)} %seeds_ref.5), channel_id=1, source_target_pairs={{2,0},{3,1},{4,2},{5,3},{6,4},{7,5},{8,6},{9,7},{10,8},{11,9},{12,... | collective-permute-start | bytes 393224 | tf_op jit(solution)/shard_map/ppermute | solution.py:123
  21.1 16.8 %collective-permute-start.2 = (f32[64,512]{1,0:T(8,128)}, f32[64,512]{1,0:T(8,128)S(1)}, u32[]{:S(2)}, u32[]{:S(2)}) collective-permute-start(f32[64,512]{1,0:T(8,128)} %seeds_ref.5), channel_id=1, source_target_pairs={{1,0},{2,1},{3,2},{4,3},{5,4},{6,5},{7,6},{8,7},{9,8},{10,9},{11,1... | collective-permute-start | bytes 393224 | tf_op jit(solution)/shard_map/ppermute | solution.py:123
  23.7 14.3 %collective-permute-start.1 = (f32[64,512]{1,0:T(8,128)}, f32[64,512]{1,0:T(8,128)S(1)}, u32[]{:S(2)}, u32[]{:S(2)}) collective-permute-start(f32[64,512]{1,0:T(8,128)} %seeds_ref.5), channel_id=1, source_target_pairs={{0,1},{1,2},{2,3},{3,4},{4,5},{5,6},{6,7},{7,8},{8,9},{9,10},{10,1... | collective-permute-start | bytes 393224 | tf_op jit(solution)/shard_map/ppermute | solution.py:123
  27.6 14.5 %collective-permute-start = (f32[64,512]{1,0:T(8,128)}, f32[64,512]{1,0:T(8,128)S(1)}, u32[]{:S(2)}, u32[]{:S(2)}) collective-permute-start(f32[64,512]{1,0:T(8,128)} %seeds_ref.5), channel_id=1, source_target_pairs={{0,2},{1,3},{2,4},{3,5},{4,6},{5,7},{6,8},{7,9},{8,10},{9,11},{10,... | collective-permute-start | bytes 393224 | tf_op jit(solution)/shard_map/ppermute | solution.py:123
  42.1 0.9 copy-start
  43.0 28.8 %copy-start.1 = (f32[64,512]{1,0:T(8,128)S(1)}, f32[64,512]{1,0:T(8,128)}, u32[]{:S(2)}) copy-start(f32[64,512]{1,0:T(8,128)} %seeds_ref.5) | copy-start | bytes 393220
  44.6 14.8 %collective-permute-start.7 = (f32[64,512]{1,0:T(8,128)S(1)}, f32[64,512]{1,0:T(8,128)S(1)}, u32[]{:S(2)}, u32[]{:S(2)}) collective-permute-start(f32[64,512]{1,0:T(8,128)S(1)} %apply.3.refs_2_), channel_id=1, source_target_pairs={{2,0},{3,1},{4,2},{5,3},{6,4},{7,5},{8,6},{9,7},{10,8},{11,9},{12,... | collective-permute-start | bytes 393224 | tf_op jit(solution)/shard_map/ppermute | solution.py:123
  51.1 8.4 %collective-permute-start.6 = (f32[64,512]{1,0:T(8,128)S(1)}, f32[64,512]{1,0:T(8,128)S(1)}, u32[]{:S(2)}, u32[]{:S(2)}) collective-permute-start(f32[64,512]{1,0:T(8,128)S(1)} %apply.3.refs_2_), channel_id=1, source_target_pairs={{1,0},{2,1},{3,2},{4,3},{5,4},{6,5},{7,6},{8,7},{9,8},{10,9},{11,1... | collective-permute-start | bytes 393224 | tf_op jit(solution)/shard_map/ppermute | solution.py:123
  53.4 6.1 %collective-permute-start.5 = (f32[64,512]{1,0:T(8,128)S(1)}, f32[64,512]{1,0:T(8,128)S(1)}, u32[]{:S(2)}, u32[]{:S(2)}) collective-permute-start(f32[64,512]{1,0:T(8,128)S(1)} %apply.3.refs_2_), channel_id=1, source_target_pairs={{0,1},{1,2},{2,3},{3,4},{4,5},{5,6},{6,7},{7,8},{8,9},{9,10},{10,1... | collective-permute-start | bytes 393224 | tf_op jit(solution)/shard_map/ppermute | solution.py:123
  57.5 14.3 %collective-permute-start.4 = (f32[64,512]{1,0:T(8,128)S(1)}, f32[64,512]{1,0:T(8,128)S(1)}, u32[]{:S(2)}, u32[]{:S(2)}) collective-permute-start(f32[64,512]{1,0:T(8,128)S(1)} %apply.3.refs_2_), channel_id=1, source_target_pairs={{0,2},{1,3},{2,4},{3,5},{4,6},{5,7},{6,8},{7,9},{8,10},{9,11},{10,... | collective-permute-start | bytes 393224 | tf_op jit(solution)/shard_map/ppermute | solution.py:123
  73.5 13.9 %collective-permute-start.11 = (f32[64,512]{1,0:T(8,128)S(1)}, f32[64,512]{1,0:T(8,128)S(1)}, u32[]{:S(2)}, u32[]{:S(2)}) collective-permute-start(f32[64,512]{1,0:T(8,128)S(1)} %apply.4.refs_2_), channel_id=1, source_target_pairs={{2,0},{3,1},{4,2},{5,3},{6,4},{7,5},{8,6},{9,7},{10,8},{11,9},{12,... | collective-permute-start | bytes 393224 | tf_op jit(solution)/shard_map/ppermute | solution.py:123
  76.1 11.3 %collective-permute-start.10 = (f32[64,512]{1,0:T(8,128)S(1)}, f32[64,512]{1,0:T(8,128)S(1)}, u32[]{:S(2)}, u32[]{:S(2)}) collective-permute-start(f32[64,512]{1,0:T(8,128)S(1)} %apply.4.refs_2_), channel_id=1, source_target_pairs={{1,0},{2,1},{3,2},{4,3},{5,4},{6,5},{7,6},{8,7},{9,8},{10,9},{11,1... | collective-permute-start | bytes 393224 | tf_op jit(solution)/shard_map/ppermute | solution.py:123
  78.0 9.4 %collective-permute-start.9 = (f32[64,512]{1,0:T(8,128)S(1)}, f32[64,512]{1,0:T(8,128)S(1)}, u32[]{:S(2)}, u32[]{:S(2)}) collective-permute-start(f32[64,512]{1,0:T(8,128)S(1)} %apply.4.refs_2_), channel_id=1, source_target_pairs={{0,1},{1,2},{2,3},{3,4},{4,5},{5,6},{6,7},{7,8},{8,9},{9,10},{10,1... | collective-permute-start | bytes 393224 | tf_op jit(solution)/shard_map/ppermute | solution.py:123
  82.6 12.9 %collective-permute-start.8 = (f32[64,512]{1,0:T(8,128)S(1)}, f32[64,512]{1,0:T(8,128)S(1)}, u32[]{:S(2)}, u32[]{:S(2)}) collective-permute-start(f32[64,512]{1,0:T(8,128)S(1)} %apply.4.refs_2_), channel_id=1, source_target_pairs={{0,2},{1,3},{2,4},{3,5},{4,6},{5,7},{6,8},{7,9},{8,10},{9,11},{10,... | collective-permute-start | bytes 393224 | tf_op jit(solution)/shard_map/ppermute | solution.py:123

commit v2 on v1

--- a/solution.py
+++ b/solution.py
@@ -85,19 +85,20 @@
         out_shape=(out, out),
         scratch_shapes=[pltpu.VMEM((events, LANES), jnp.float32)] * 4,
         compiler_params=pltpu.CompilerParams(vmem_limit_bytes=32 * 2**20),
+        cost_estimate=pl.CostEstimate(flops=8 * 32 * events * SPAN * 4, bytes_accessed=4 * events * SPAN, transcendentals=0),
         name="build",
     )(edges)
 
 
-def apply_kernel(high_ref, low_ref, seeds_ref, *refs):
-    *panel_refs, out_ref, window_ref = refs
+def apply_kernel(high_ref, low_ref, seeds_ref, own_ref, pair_ref, far_ref, cross_ref, out_ref, window_ref):
     channels, events = out_ref.shape
-    for number, ref in enumerate(panel_refs):
-        value = ref[...]
+    second = lax.axis_index("cols") % 2
+    blocks = [own_ref[...], pair_ref[...], cross_ref[...], far_ref[:channels], far_ref[channels:]]
+    for value, place in zip(blocks, (2, 3, 4, 1, 0)):
+        at = pl.multiple_of((place + second * (4 - 2 * place)) * events, events)
         high = value.astype(jnp.bfloat16)
-        columns = slice(number * events, (number + 1) * events)
-        window_ref[:channels, columns] = high
-        window_ref[channels:, columns] = (value - high.astype(jnp.float32)).astype(jnp.bfloat16)
+        window_ref[:channels, pl.ds(at, events)] = high
+        window_ref[channels:, pl.ds(at, events)] = (value - high.astype(jnp.float32)).astype(jnp.bfloat16)
     for part in range(events // BLOCK):
         rows = slice(part * BLOCK, (part + 1) * BLOCK)
         window = window_ref[:, part * BLOCK:part * BLOCK + SPAN]
@@ -112,27 +113,41 @@
     return pl.pallas_call(
         apply_kernel,
         out_shape=jax.ShapeDtypeStruct(seeds.shape, jnp.float32),
-        scratch_shapes=[pltpu.VMEM((2 * channels, len(panels) * events), jnp.bfloat16)],
+        scratch_shapes=[pltpu.VMEM((2 * channels, 5 * events), jnp.bfloat16)],
         compiler_params=pltpu.CompilerParams(vmem_limit_bytes=32 * 2**20),
+        cost_estimate=pl.CostEstimate(flops=6 * channels * events * SPAN, bytes_accessed=4 * events * SPAN, transcendentals=0),
         name="apply",
     )(*matrix, seeds, *panels)
 
 
-def shifted(cells, step, count):
-    pairs = [(i, i + step) for i in range(count) if 0 <= i + step < count]
-    return lax.ppermute(cells, AXES, pairs)
+def pack_kernel(offsets_ref, weights_ref, out_ref):
+    slots = offsets_ref.shape[0]
+    out_ref[:slots] = offsets_ref[...].astype(jnp.float32)
+    out_ref[slots:] = weights_ref[...]
+
+
+def pack(offsets, weights):
+    slots, events = offsets.shape
+    return pl.pallas_call(
+        pack_kernel,
+        out_shape=jax.ShapeDtypeStruct((2 * slots, events), jnp.float32),
+        name="pack",
+    )(offsets, weights)
 
 
 def on_device(offsets, weights, seeds, *, count):
-    reach = HW // seeds.shape[1]
-    edges = jnp.concatenate([offsets.astype(jnp.float32), weights], axis=0)
+    channels = seeds.shape[0]
+    on_chip = [(i, i ^ 1) for i in range(count)]
+    off_chip = [(i, i + 1 if i % 2 else i - 1) for i in range(1, count - 1)]
+    edges = pack(offsets, weights)
     edges = lax.all_to_all(edges, "cols", split_axis=1, concat_axis=0, tiled=True)
     matrix = build(edges)
     scores = seeds
     for _ in range(ITERS):
-        before = [shifted(scores, step, count) for step in range(reach, 0, -1)]
-        after = [shifted(scores, -step, count) for step in range(1, reach + 1)]
-        scores = apply(matrix, seeds, [*before, scores, *after])
+        pair = lax.ppermute(scores, AXES, on_chip)
+        far = lax.ppermute(jnp.concatenate([scores, pair], axis=0), AXES, off_chip)
+        cross = lax.ppermute(far[:channels], AXES, on_chip)
+        scores = apply(matrix, seeds, [scores, pair, far, cross])
     return scores
 
 

time: 98.3 us -> 78.8 us (0.80)
  starting transfers between devices: 55.8 us -> 36.1 us
  Pallas kernels: 13.8 us -> 15.4 us
  other arithmetic: 2.38 us -> 0.96 us
  waiting for transfers between devices: 24.7 us -> 26 us
    ppermute x12 -> x9, starting transfers between devices: 47.5 us -> 25.5 us  [the longest x3 13.8 us: on_device(): cross = lax.ppermute(far[:channels], AXES, on_chip)]
    all_to_all x1, waiting for transfers between devices: 0.01 us -> 7.81 us  [on_device(): lax.all_to_all(edges, 'cols', split_axis=1, concat_axis=0, tiled=True)]
    ppermute x12 -> x9, waiting for transfers between devices: 24.7 us -> 18.2 us  [the longest x3 13.1 us: on_device(): far = lax.ppermute(jnp.concatenate([scores, pair], axis=0), AXES, off_chip)]
    all_to_all x1, starting transfers between devices: 8.24 us -> 10.6 us  [on_device(): lax.all_to_all(edges, 'cols', split_axis=1, concat_axis=0, tiled=True)]
    pallas_call x0 -> x1, Pallas kernels: none -> 1.55 us  [pack(): pl.pallas_call(pack_kernel, out_shape=jax.ShapeDtypeStruct((2 * slots, ev...]
  transfers between devices with their start and end apart: 13 -> 10, of which waited for: 3 -> 8; matrix products, arithmetic and copies ran while one was open for 0% -> 0% of each run, Pallas kernels for 9% -> 13%
where the time goes in v2:
time: 78.8 us; the launch traced here: 78.5 us
  starting transfers between devices  36.1 us (46%)
  waiting for transfers between devices  26 us (33%)
  Pallas kernels  15.4 us (20%)
  other arithmetic  0.96 us (1%)
    ppermute x3, starting transfers between devices, on_device(): cross = lax.ppermute(far[:channels], AXES, on_chip)  13.8 us
    ppermute x3, waiting for transfers between devices, on_device(): far = lax.ppermute(jnp.concatenate([scores, pair], axis=0), AXES, off_chip)  13.1 us
    all_to_all x1, starting transfers between devices, on_device(): lax.all_to_all(edges, 'cols', split_axis=1, concat_axis=0, tiled=True)  10.6 us
    ppermute x3, starting transfers between devices, on_device(): far = lax.ppermute(jnp.concatenate([scores, pair], axis=0), AXES, off_chip)  9.26 us
    pallas_call x1, Pallas kernels, build(): pl.pallas_call(build_kernel, out_shape=(out, out), scratch_shapes=[pltpu....  8.39 us
    all_to_all x1, waiting for transfers between devices, on_device(): lax.all_to_all(edges, 'cols', split_axis=1, concat_axis=0, tiled=True)  7.81 us
    pallas_call x3, Pallas kernels, apply(): pl.pallas_call(apply_kernel, out_shape=jax.ShapeDtypeStruct(seeds.shape,...  5.42 us
    ppermute x3, waiting for transfers between devices, on_device(): pair = lax.ppermute(scores, AXES, on_chip)  3.17 us
  transfers between devices with their start and end apart: 10, of which 8 were waited for; matrix products, arithmetic and copies ran while one was open for 0% of the time, Pallas kernels for 13%

profile of v2, /device:TPU:33, one launch (start us, length us, event | category | flops | bytes accessed | tf_op | source)
XLA Modules:
  0.0 78.5 jit_solution(6625995911890018070)
XLA Ops:
  0.0 0.7 collective-permute-start
  0.7 1.2 %collective-permute-done.pair_ref = f32[64,512]{1,0:T(8,128)S(1)} collective-permute-done((f32[64,512]{1,0:T(8,128)}, f32[64,512]{1,0:T(8,128)S(1)}, u32[]{:S(2)}, u32[]{:S(2)}) %collective-permute-start) | collective-permute-done | bytes 131104 | tf_op jit(solution)/shard_map/ppermute | solution.py:147
  1.9 0.9 %pad_maximum_fusion = f32[128,512]{1,0:T(8,128)S(1)} fusion(f32[64,512]{1,0:T(8,128)S(1)} %collective-permute-done.pair_ref, f32[64,512]{1,0:T(8,128)} %seeds_ref.5), kind=kLoop, calls=%fused_computation | loop fusion | flops 65536 | bytes 524288 | tf_op jit(solution)/shard_map/concatenate | solution.py:148
  2.8 5.1 %collective-permute-start.1 = (f32[128,512]{1,0:T(8,128)S(1)}, f32[128,512]{1,0:T(8,128)S(1)}, u32[]{:S(2)}, u32[]{:S(2)}) collective-permute-start(f32[128,512]{1,0:T(8,128)S(1)} %pad_maximum_fusion), channel_id=1, source_target_pairs={{1,2},{2,1},{3,4},{4,3},{5,6},{6,5},{7,8},{8,7},{9,10},{10,9},{11,... | collective-permute-start | bytes 786440 | tf_op jit(solution)/shard_map/ppermute | solution.py:148
  8.0 1.5 %pack.1 = f32[8,4096]{1,0:T(8,128)} custom-call(s32[4,4096]{1,0:T(4,128)} %offsets_ref.1, f32[4,4096]{1,0:T(4,128)} %weights_ref.1), custom_call_target="tpu_custom_call" | custom-call | tf_op jit(solution)/shard_map/pack/pallas_call | solution.py:131
  9.5 10.6 %all-to-all-start = ((f32[8,8,512]{2,0,1:T(8,128)}), f32[8,8,512]{2,0,1:T(8,128)S(1)}, u32[]{:S(2)}, u32[]{:S(2)}) async-start(f32[8,8,512]{2,0,1:T(8,128)} %bitcast.5), calls=%async_computation | async-start | bytes 262144 | tf_op jit(solution)/shard_map/all_to_all | solution.py:143
  20.1 0.0 copy-start
  20.1 0.0 collective-permute-done.1.far_ref
  20.2 0.2 collective-permute-start.2
  20.4 7.8 %all-to-all-done = f32[8,8,512]{2,0,1:T(8,128)S(1)} async-done(((f32[8,8,512]{2,0,1:T(8,128)}), f32[8,8,512]{2,0,1:T(8,128)S(1)}, u32[]{:S(2)}, u32[]{:S(2)}) %all-to-all-start) | async-done | bytes 131104 | tf_op jit(solution)/shard_map/all_to_all | solution.py:143
  28.2 8.4 %build.1 = (bf16[512,2304]{1,0:T(8,128)(2,1)S(1)}, bf16[512,2304]{1,0:T(8,128)(2,1)S(1)}) custom-call(f32[64,512]{1,0:T(8,128)S(1)} %bitcast.4), custom_call_target="tpu_custom_call" | custom-call | flops 1207959552 | bytes 4718592 | tf_op jit(solution)/shard_map/build/pallas_call | solution.py:83
  36.6 0.0 collective-permute-done.2.cross_ref
  36.6 0.0 copy-done
  36.6 1.6 %apply.3.own_ref = f32[64,512]{1,0:T(8,128)S(1)} custom-call(bf16[512,2304]{1,0:T(8,128)(2,1)S(1)} %get-tuple-element.7.high_ref, bf16[512,2304]{1,0:T(8,128)(2,1)S(1)} %get-tuple-element.8.low_ref, f32[64,512]{1,0:T(8,128)S(1)} %copy-done, f32[64,512]{1,0:T(8,128)S(1)} %copy-done, f32[64,512]{1,0:T(8,128)S(1)} %collective-permute-done.pair_ref, ...), custom_call_target="tpu_custom_call" | custom-call | flops 452984832 | bytes 4718592 | tf_op jit(solution)/shard_map/apply/pallas_call | solution.py:113
  38.2 1.3 %collective-permute-start.3 = (f32[64,512]{1,0:T(8,128)S(1)}, f32[64,512]{1,0:T(8,128)S(1)}, u32[]{:S(2)}, u32[]{:S(2)}) collective-permute-start(f32[64,512]{1,0:T(8,128)S(1)} %apply.3.own_ref), channel_id=1, source_target_pairs={{0,1},{1,0},{2,3},{3,2},{4,5},{5,4},{6,7},{7,6},{8,9},{9,8},{10,11... | collective-permute-start | bytes 393224 | tf_op jit(solution)/shard_map/ppermute | solution.py:147
  39.5 1.0 %collective-permute-done.3.pair_ref = f32[64,512]{1,0:T(8,128)S(1)} collective-permute-done((f32[64,512]{1,0:T(8,128)S(1)}, f32[64,512]{1,0:T(8,128)S(1)}, u32[]{:S(2)}, u32[]{:S(2)}) %collective-permute-start.3) | collective-permute-done | bytes 131104 | tf_op jit(solution)/shard_map/ppermute | solution.py:147
  40.5 2.2 %collective-permute-start.4 = (f32[128,512]{1,0:T(8,128)S(1)}, f32[128,512]{1,0:T(8,128)S(1)}, u32[]{:S(2)}, u32[]{:S(2)}) collective-permute-start(f32[128,512]{1,0:T(8,128)S(1)} %pad_maximum_fusion.1), channel_id=1, source_target_pairs={{1,2},{2,1},{3,4},{4,3},{5,6},{6,5},{7,8},{8,7},{9,10},{10,9},{11,... | collective-permute-start | bytes 786440 | tf_op jit(solution)/shard_map/ppermute | solution.py:148
  42.7 6.4 %collective-permute-done.4.far_ref = f32[128,512]{1,0:T(8,128)S(1)} collective-permute-done((f32[128,512]{1,0:T(8,128)S(1)}, f32[128,512]{1,0:T(8,128)S(1)}, u32[]{:S(2)}, u32[]{:S(2)}) %collective-permute-start.4) | collective-permute-done | bytes 262176 | tf_op jit(solution)/shard_map/ppermute | solution.py:148
  49.1 6.8 %collective-permute-start.5 = (f32[64,512]{1,0:T(8,128)S(1)}, f32[64,512]{1,0:T(8,128)S(1)}, u32[]{:S(2)}, u32[]{:S(2)}) collective-permute-start(f32[64,512]{1,0:T(8,128)S(1)} %slice.13), channel_id=1, source_target_pairs={{0,1},{1,0},{2,3},{3,2},{4,5},{5,4},{6,7},{7,6},{8,9},{9,8},{10,11... | collective-permute-start | bytes 393224 | tf_op jit(solution)/shard_map/ppermute | solution.py:149
  55.9 1.0 %collective-permute-done.5.cross_ref = f32[64,512]{1,0:T(8,128)S(1)} collective-permute-done((f32[64,512]{1,0:T(8,128)S(1)}, f32[64,512]{1,0:T(8,128)S(1)}, u32[]{:S(2)}, u32[]{:S(2)}) %collective-permute-start.5) | collective-permute-done | bytes 131104 | tf_op jit(solution)/shard_map/ppermute | solution.py:149
  56.9 1.6 %apply.4.own_ref = f32[64,512]{1,0:T(8,128)S(1)} custom-call(bf16[512,2304]{1,0:T(8,128)(2,1)S(1)} %get-tuple-element.7.high_ref, bf16[512,2304]{1,0:T(8,128)(2,1)S(1)} %get-tuple-element.8.low_ref, f32[64,512]{1,0:T(8,128)S(1)} %copy-done, f32[64,512]{1,0:T(8,128)S(1)} %apply.3.own_ref, f32[64,512]{1,0:T(8,128)S(1)} %collective-permute-done.3.pair_ref, ...), custom_call_target="tpu_custom_call" | custom-call | flops 452984832 | bytes 4718592 | tf_op jit(solution)/shard_map/apply/pallas_call | solution.py:113
  58.5 0.5 collective-permute-start.6
  58.9 1.0 %collective-permute-done.6.pair_ref = f32[64,512]{1,0:T(8,128)S(1)} collective-permute-done((f32[64,512]{1,0:T(8,128)S(1)}, f32[64,512]{1,0:T(8,128)S(1)}, u32[]{:S(2)}, u32[]{:S(2)}) %collective-permute-start.6) | collective-permute-done | bytes 131104 | tf_op jit(solution)/shard_map/ppermute | solution.py:147
  59.9 1.9 %collective-permute-start.7 = (f32[128,512]{1,0:T(8,128)S(1)}, f32[128,512]{1,0:T(8,128)S(1)}, u32[]{:S(2)}, u32[]{:S(2)}) collective-permute-start(f32[128,512]{1,0:T(8,128)S(1)} %pad_maximum_fusion.2), channel_id=1, source_target_pairs={{1,2},{2,1},{3,4},{4,3},{5,6},{6,5},{7,8},{8,7},{9,10},{10,9},{11,... | collective-permute-start | bytes 786440 | tf_op jit(solution)/shard_map/ppermute | solution.py:148
  61.9 6.7 %collective-permute-done.7.far_ref = f32[128,512]{1,0:T(8,128)S(1)} collective-permute-done((f32[128,512]{1,0:T(8,128)S(1)}, f32[128,512]{1,0:T(8,128)S(1)}, u32[]{:S(2)}, u32[]{:S(2)}) %collective-permute-start.7) | collective-permute-done | bytes 262176 | tf_op jit(solution)/shard_map/ppermute | solution.py:148
  68.5 6.8 %collective-permute-start.8 = (f32[64,512]{1,0:T(8,128)S(1)}, f32[64,512]{1,0:T(8,128)S(1)}, u32[]{:S(2)}, u32[]{:S(2)}) collective-permute-start(f32[64,512]{1,0:T(8,128)S(1)} %slice.14), channel_id=1, source_target_pairs={{0,1},{1,0},{2,3},{3,2},{4,5},{5,4},{6,7},{7,6},{8,9},{9,8},{10,11... | collective-permute-start | bytes 393224 | tf_op jit(solution)/shard_map/ppermute | solution.py:149
  75.3 1.0 %collective-permute-done.8.cross_ref = f32[64,512]{1,0:T(8,128)S(1)} collective-permute-done((f32[64,512]{1,0:T(8,128)S(1)}, f32[64,512]{1,0:T(8,128)S(1)}, u32[]{:S(2)}, u32[]{:S(2)}) %collective-permute-start.8) | collective-permute-done | bytes 131104 | tf_op jit(solution)/shard_map/ppermute | solution.py:149
  76.3 2.2 %apply.5 = f32[64,512]{1,0:T(8,128)} custom-call(bf16[512,2304]{1,0:T(8,128)(2,1)S(1)} %get-tuple-element.7.high_ref, bf16[512,2304]{1,0:T(8,128)(2,1)S(1)} %get-tuple-element.8.low_ref, f32[64,512]{1,0:T(8,128)S(1)} %copy-done, f32[64,512]{1,0:T(8,128)S(1)} %apply.4.own_ref, f32[64,512]{1,0:T(8,128)S(1)} %collective-permute-done.6.pair_ref, ...), custom_call_target="tpu_custom_call" | custom-call | flops 452984832 | bytes 4718592 | tf_op jit(solution)/shard_map/apply/pallas_call | solution.py:113
  (5 shorter events, 0.1 us)
Async XLA Ops:
  0.0 1.9 %collective-permute-start = (f32[64,512]{1,0:T(8,128)}, f32[64,512]{1,0:T(8,128)S(1)}, u32[]{:S(2)}, u32[]{:S(2)}) collective-permute-start(f32[64,512]{1,0:T(8,128)} %seeds_ref.5), channel_id=1, source_target_pairs={{0,1},{1,0},{2,3},{3,2},{4,5},{5,4},{6,7},{7,6},{8,9},{9,8},{10,11... | collective-permute-start | bytes 393224 | tf_op jit(solution)/shard_map/ppermute | solution.py:147
  2.8 17.3 %collective-permute-start.1 = (f32[128,512]{1,0:T(8,128)S(1)}, f32[128,512]{1,0:T(8,128)S(1)}, u32[]{:S(2)}, u32[]{:S(2)}) collective-permute-start(f32[128,512]{1,0:T(8,128)S(1)} %pad_maximum_fusion), channel_id=1, source_target_pairs={{1,2},{2,1},{3,4},{4,3},{5,6},{6,5},{7,8},{8,7},{9,10},{10,9},{11,... | collective-permute-start | bytes 786440 | tf_op jit(solution)/shard_map/ppermute | solution.py:148
  9.5 18.7 %all-to-all-start = ((f32[8,8,512]{2,0,1:T(8,128)}), f32[8,8,512]{2,0,1:T(8,128)S(1)}, u32[]{:S(2)}, u32[]{:S(2)}) async-start(f32[8,8,512]{2,0,1:T(8,128)} %bitcast.5), calls=%async_computation | async-start | bytes 262144 | tf_op jit(solution)/shard_map/all_to_all | solution.py:143
  20.1 16.5 %copy-start = (f32[64,512]{1,0:T(8,128)S(1)}, f32[64,512]{1,0:T(8,128)}, u32[]{:S(2)}) copy-start(f32[64,512]{1,0:T(8,128)} %seeds_ref.5) | copy-start | bytes 393220
  20.2 16.4 %collective-permute-start.2 = (f32[64,512]{1,0:T(8,128)S(1)}, f32[64,512]{1,0:T(8,128)S(1)}, u32[]{:S(2)}, u32[]{:S(2)}) collective-permute-start(f32[64,512]{1,0:T(8,128)S(1)} %slice.12), channel_id=1, source_target_pairs={{0,1},{1,0},{2,3},{3,2},{4,5},{5,4},{6,7},{7,6},{8,9},{9,8},{10,11... | collective-permute-start | bytes 393224 | tf_op jit(solution)/shard_map/ppermute | solution.py:149
  38.2 2.3 %collective-permute-start.3 = (f32[64,512]{1,0:T(8,128)S(1)}, f32[64,512]{1,0:T(8,128)S(1)}, u32[]{:S(2)}, u32[]{:S(2)}) collective-permute-start(f32[64,512]{1,0:T(8,128)S(1)} %apply.3.own_ref), channel_id=1, source_target_pairs={{0,1},{1,0},{2,3},{3,2},{4,5},{5,4},{6,7},{7,6},{8,9},{9,8},{10,11... | collective-permute-start | bytes 393224 | tf_op jit(solution)/shard_map/ppermute | solution.py:147
  40.5 8.6 %collective-permute-start.4 = (f32[128,512]{1,0:T(8,128)S(1)}, f32[128,512]{1,0:T(8,128)S(1)}, u32[]{:S(2)}, u32[]{:S(2)}) collective-permute-start(f32[128,512]{1,0:T(8,128)S(1)} %pad_maximum_fusion.1), channel_id=1, source_target_pairs={{1,2},{2,1},{3,4},{4,3},{5,6},{6,5},{7,8},{8,7},{9,10},{10,9},{11,... | collective-permute-start | bytes 786440 | tf_op jit(solution)/shard_map/ppermute | solution.py:148
  49.1 7.8 %collective-permute-start.5 = (f32[64,512]{1,0:T(8,128)S(1)}, f32[64,512]{1,0:T(8,128)S(1)}, u32[]{:S(2)}, u32[]{:S(2)}) collective-permute-start(f32[64,512]{1,0:T(8,128)S(1)} %slice.13), channel_id=1, source_target_pairs={{0,1},{1,0},{2,3},{3,2},{4,5},{5,4},{6,7},{7,6},{8,9},{9,8},{10,11... | collective-permute-start | bytes 393224 | tf_op jit(solution)/shard_map/ppermute | solution.py:149
  58.5 1.4 %collective-permute-start.6 = (f32[64,512]{1,0:T(8,128)S(1)}, f32[64,512]{1,0:T(8,128)S(1)}, u32[]{:S(2)}, u32[]{:S(2)}) collective-permute-start(f32[64,512]{1,0:T(8,128)S(1)} %apply.4.own_ref), channel_id=1, source_target_pairs={{0,1},{1,0},{2,3},{3,2},{4,5},{5,4},{6,7},{7,6},{8,9},{9,8},{10,11... | collective-permute-start | bytes 393224 | tf_op jit(solution)/shard_map/ppermute | solution.py:147
  59.9 8.6 %collective-permute-start.7 = (f32[128,512]{1,0:T(8,128)S(1)}, f32[128,512]{1,0:T(8,128)S(1)}, u32[]{:S(2)}, u32[]{:S(2)}) collective-permute-start(f32[128,512]{1,0:T(8,128)S(1)} %pad_maximum_fusion.2), channel_id=1, source_target_pairs={{1,2},{2,1},{3,4},{4,3},{5,6},{6,5},{7,8},{8,7},{9,10},{10,9},{11,... | collective-permute-start | bytes 786440 | tf_op jit(solution)/shard_map/ppermute | solution.py:148
  68.5 7.8 %collective-permute-start.8 = (f32[64,512]{1,0:T(8,128)S(1)}, f32[64,512]{1,0:T(8,128)S(1)}, u32[]{:S(2)}, u32[]{:S(2)}) collective-permute-start(f32[64,512]{1,0:T(8,128)S(1)} %slice.14), channel_id=1, source_target_pairs={{0,1},{1,0},{2,3},{3,2},{4,5},{5,4},{6,7},{7,6},{8,9},{9,8},{10,11... | collective-permute-start | bytes 393224 | tf_op jit(solution)/shard_map/ppermute | solution.py:149

commit v3 on v2

--- a/solution.py
+++ b/solution.py
@@ -74,7 +74,7 @@
             low_ref[pl.ds(at, 16), columns] = (both - high.astype(jnp.float32)).astype(jnp.bfloat16)
         return 0
 
-    lax.fori_loop(0, events // 16, sixteen, 0)
+    lax.fori_loop(0, events // 16, sixteen, 0, unroll=8)
 
 
 def build(edges):
@@ -85,7 +85,7 @@
         out_shape=(out, out),
         scratch_shapes=[pltpu.VMEM((events, LANES), jnp.float32)] * 4,
         compiler_params=pltpu.CompilerParams(vmem_limit_bytes=32 * 2**20),
-        cost_estimate=pl.CostEstimate(flops=8 * 32 * events * SPAN * 4, bytes_accessed=4 * events * SPAN, transcendentals=0),
+        cost_estimate=pl.CostEstimate(flops=3000000000, bytes_accessed=4 * events * SPAN, transcendentals=0),
         name="build",
     )(edges)
 
@@ -143,9 +143,11 @@
     edges = lax.all_to_all(edges, "cols", split_axis=1, concat_axis=0, tiled=True)
     matrix = build(edges)
     scores = seeds
-    for _ in range(ITERS):
+    for step in range(ITERS):
         pair = lax.ppermute(scores, AXES, on_chip)
         far = lax.ppermute(jnp.concatenate([scores, pair], axis=0), AXES, off_chip)
+        if step == 0:
+            far, *matrix = lax.optimization_barrier((far, *matrix))
         cross = lax.ppermute(far[:channels], AXES, on_chip)
         scores = apply(matrix, seeds, [scores, pair, far, cross])
     return scores

time: 78.8 us -> 70.1 us (0.89)
  Pallas kernels: 15.4 us -> 10.5 us
  starting transfers between devices: 36.1 us -> 32.8 us
    all_to_all x1, waiting for transfers between devices: 7.81 us -> 2.76 us  [on_device(): lax.all_to_all(edges, 'cols', split_axis=1, concat_axis=0, tiled=True)]
    pallas_call x1, Pallas kernels: 8.39 us -> 3.5 us  [build(): pl.pallas_call(build_kernel, out_shape=(out, out), scratch_shapes=[pltpu....]
    ppermute x3, waiting for transfers between devices: 13.1 us -> 17.8 us  [on_device(): far = lax.ppermute(jnp.concatenate([scores, pair], axis=0), AXES, off_chip)]
    all_to_all x1, starting transfers between devices: 10.6 us -> 7.68 us  [on_device(): lax.all_to_all(edges, 'cols', split_axis=1, concat_axis=0, tiled=True)]
    ppermute x3, starting transfers between devices: 13.8 us -> 15.2 us  [on_device(): cross = lax.ppermute(far[:channels], AXES, on_chip)]
    ppermute x3, waiting for transfers between devices: 3.17 us -> 1.98 us  [on_device(): pair = lax.ppermute(scores, AXES, on_chip)]
    ppermute x3, waiting for transfers between devices: 1.98 us -> 2.96 us  [on_device(): cross = lax.ppermute(far[:channels], AXES, on_chip)]
    ppermute x3, starting transfers between devices: 9.26 us -> 8.28 us  [on_device(): far = lax.ppermute(jnp.concatenate([scores, pair], axis=0), AXES, off_chip)]
  transfers between devices with their start and end apart: 10 -> 10, of which waited for: 8 -> 8; matrix products, arithmetic and copies ran while one was open for 0% -> 1% of each run, Pallas kernels for 13% -> 7%
where the time goes in v3:
time: 70.1 us; the launch traced here: 69.8 us
  starting transfers between devices  32.8 us (47%)
  waiting for transfers between devices  25.5 us (36%)
  Pallas kernels  10.5 us (15%)
  other arithmetic  0.96 us (1%)
    ppermute x3, waiting for transfers between devices, on_device(): far = lax.ppermute(jnp.concatenate([scores, pair], axis=0), AXES, off_chip)  17.8 us
    ppermute x3, starting transfers between devices, on_device(): cross = lax.ppermute(far[:channels], AXES, on_chip)  15.2 us
    ppermute x3, starting transfers between devices, on_device(): far = lax.ppermute(jnp.concatenate([scores, pair], axis=0), AXES, off_chip)  8.28 us
    all_to_all x1, starting transfers between devices, on_device(): lax.all_to_all(edges, 'cols', split_axis=1, concat_axis=0, tiled=True)  7.68 us
    pallas_call x3, Pallas kernels, apply(): pl.pallas_call(apply_kernel, out_shape=jax.ShapeDtypeStruct(seeds.shape,...  5.43 us
    pallas_call x1, Pallas kernels, build(): pl.pallas_call(build_kernel, out_shape=(out, out), scratch_shapes=[pltpu....  3.5 us
    ppermute x3, waiting for transfers between devices, on_device(): cross = lax.ppermute(far[:channels], AXES, on_chip)  2.96 us
    all_to_all x1, waiting for transfers between devices, on_device(): lax.all_to_all(edges, 'cols', split_axis=1, concat_axis=0, tiled=True)  2.76 us
  transfers between devices with their start and end apart: 10, of which 8 were waited for; matrix products, arithmetic and copies ran while one was open for 1% of the time, Pallas kernels for 7%

profile of v3, /device:TPU:33, one launch (start us, length us, event | category | flops | bytes accessed | tf_op | source)
XLA Modules:
  0.0 69.8 jit_solution(12924725638612195085)
XLA Ops:
  0.0 0.7 collective-permute-start
  0.7 1.5 %pack.1 = f32[8,4096]{1,0:T(8,128)} custom-call(s32[4,4096]{1,0:T(4,128)} %offsets_ref.1, f32[4,4096]{1,0:T(4,128)} %weights_ref.1), custom_call_target="tpu_custom_call" | custom-call | tf_op jit(solution)/shard_map/pack/pallas_call | solution.py:131
  2.2 7.7 %all-to-all-start = ((f32[8,8,512]{2,0,1:T(8,128)}), f32[8,8,512]{2,0,1:T(8,128)S(1)}, u32[]{:S(2)}, u32[]{:S(2)}) async-start(f32[8,8,512]{2,0,1:T(8,128)} %bitcast.5), calls=%async_computation | async-start | bytes 262144 | tf_op jit(solution)/shard_map/all_to_all | solution.py:143
  9.9 0.0 collective-permute-done.pair_ref
  9.9 0.9 %pad_maximum_fusion = f32[128,512]{1,0:T(8,128)S(1)} fusion(f32[64,512]{1,0:T(8,128)S(1)} %collective-permute-done.pair_ref, f32[64,512]{1,0:T(8,128)} %seeds_ref.5), kind=kLoop, calls=%fused_computation | loop fusion | flops 65536 | bytes 524288 | tf_op jit(solution)/shard_map/concatenate | solution.py:148
  10.8 4.4 %collective-permute-start.1 = (f32[128,512]{1,0:T(8,128)S(1)}, f32[128,512]{1,0:T(8,128)S(1)}, u32[]{:S(2)}, u32[]{:S(2)}) collective-permute-start(f32[128,512]{1,0:T(8,128)S(1)} %pad_maximum_fusion), channel_id=1, source_target_pairs={{1,2},{2,1},{3,4},{4,3},{5,6},{6,5},{7,8},{8,7},{9,10},{10,9},{11,... | collective-permute-start | bytes 786440 | tf_op jit(solution)/shard_map/ppermute | solution.py:148
  15.3 2.8 %all-to-all-done = f32[8,8,512]{2,0,1:T(8,128)S(1)} async-done(((f32[8,8,512]{2,0,1:T(8,128)}), f32[8,8,512]{2,0,1:T(8,128)S(1)}, u32[]{:S(2)}, u32[]{:S(2)}) %all-to-all-start) | async-done | bytes 131104 | tf_op jit(solution)/shard_map/all_to_all | solution.py:143
  18.0 0.0 copy-start
  18.0 3.5 %build.1 = (bf16[512,2304]{1,0:T(8,128)(2,1)S(1)}, bf16[512,2304]{1,0:T(8,128)(2,1)S(1)}) custom-call(f32[64,512]{1,0:T(8,128)S(1)} %bitcast.4), custom_call_target="tpu_custom_call" | custom-call | flops 3000000000 | bytes 4718592 | tf_op jit(solution)/shard_map/build/pallas_call | solution.py:83
  21.5 0.0 collective-permute-done.1.far_ref
  21.6 5.6 %collective-permute-start.2 = (f32[64,512]{1,0:T(8,128)S(1)}, f32[64,512]{1,0:T(8,128)S(1)}, u32[]{:S(2)}, u32[]{:S(2)}) collective-permute-start(f32[64,512]{1,0:T(8,128)S(1)} %slice.9), channel_id=1, source_target_pairs={{0,1},{1,0},{2,3},{3,2},{4,5},{5,4},{6,7},{7,6},{8,9},{9,8},{10,11... | collective-permute-start | bytes 393224 | tf_op jit(solution)/shard_map/ppermute | solution.py:151
  27.2 1.0 %collective-permute-done.2.cross_ref = f32[64,512]{1,0:T(8,128)S(1)} collective-permute-done((f32[64,512]{1,0:T(8,128)S(1)}, f32[64,512]{1,0:T(8,128)S(1)}, u32[]{:S(2)}, u32[]{:S(2)}) %collective-permute-start.2) | collective-permute-done | bytes 131104 | tf_op jit(solution)/shard_map/ppermute | solution.py:151
  28.2 0.0 copy-done
  28.2 1.6 %apply.3.own_ref = f32[64,512]{1,0:T(8,128)S(1)} custom-call(bf16[512,2304]{1,0:T(8,128)(2,1)S(1)} %get-tuple-element.12.high_ref, bf16[512,2304]{1,0:T(8,128)(2,1)S(1)} %get-tuple-element.13.low_ref, f32[64,512]{1,0:T(8,128)S(1)} %copy-done, f32[64,512]{1,0:T(8,128)S(1)} %copy-done, f32[64,512]{1,0:T(8,128)S(1)} %collective-permute-done.pair_ref, ...), custom_call_target="tpu_custom_call" | custom-call | flops 452984832 | bytes 4718592 | tf_op jit(solution)/shard_map/apply/pallas_call | solution.py:113
  29.8 0.4 collective-permute-start.3
  30.2 1.0 %collective-permute-done.3.pair_ref = f32[64,512]{1,0:T(8,128)S(1)} collective-permute-done((f32[64,512]{1,0:T(8,128)S(1)}, f32[64,512]{1,0:T(8,128)S(1)}, u32[]{:S(2)}, u32[]{:S(2)}) %collective-permute-start.3) | collective-permute-done | bytes 131104 | tf_op jit(solution)/shard_map/ppermute | solution.py:147
  31.3 1.9 %collective-permute-start.4 = (f32[128,512]{1,0:T(8,128)S(1)}, f32[128,512]{1,0:T(8,128)S(1)}, u32[]{:S(2)}, u32[]{:S(2)}) collective-permute-start(f32[128,512]{1,0:T(8,128)S(1)} %pad_maximum_fusion.1), channel_id=1, source_target_pairs={{1,2},{2,1},{3,4},{4,3},{5,6},{6,5},{7,8},{8,7},{9,10},{10,9},{11,... | collective-permute-start | bytes 786440 | tf_op jit(solution)/shard_map/ppermute | solution.py:148
  33.2 9.4 %collective-permute-done.4.far_ref = f32[128,512]{1,0:T(8,128)S(1)} collective-permute-done((f32[128,512]{1,0:T(8,128)S(1)}, f32[128,512]{1,0:T(8,128)S(1)}, u32[]{:S(2)}, u32[]{:S(2)}) %collective-permute-start.4) | collective-permute-done | bytes 262176 | tf_op jit(solution)/shard_map/ppermute | solution.py:148
  42.6 4.5 %collective-permute-start.5 = (f32[64,512]{1,0:T(8,128)S(1)}, f32[64,512]{1,0:T(8,128)S(1)}, u32[]{:S(2)}, u32[]{:S(2)}) collective-permute-start(f32[64,512]{1,0:T(8,128)S(1)} %slice.12), channel_id=1, source_target_pairs={{0,1},{1,0},{2,3},{3,2},{4,5},{5,4},{6,7},{7,6},{8,9},{9,8},{10,11... | collective-permute-start | bytes 393224 | tf_op jit(solution)/shard_map/ppermute | solution.py:151
  47.1 1.0 %collective-permute-done.5.cross_ref = f32[64,512]{1,0:T(8,128)S(1)} collective-permute-done((f32[64,512]{1,0:T(8,128)S(1)}, f32[64,512]{1,0:T(8,128)S(1)}, u32[]{:S(2)}, u32[]{:S(2)}) %collective-permute-start.5) | collective-permute-done | bytes 131104 | tf_op jit(solution)/shard_map/ppermute | solution.py:151
  48.1 1.6 %apply.4.own_ref = f32[64,512]{1,0:T(8,128)S(1)} custom-call(bf16[512,2304]{1,0:T(8,128)(2,1)S(1)} %get-tuple-element.12.high_ref, bf16[512,2304]{1,0:T(8,128)(2,1)S(1)} %get-tuple-element.13.low_ref, f32[64,512]{1,0:T(8,128)S(1)} %copy-done, f32[64,512]{1,0:T(8,128)S(1)} %apply.3.own_ref, f32[64,512]{1,0:T(8,128)S(1)} %collective-permute-done.3.pair_ref, ...), custom_call_target="tpu_custom_call" | custom-call | flops 452984832 | bytes 4718592 | tf_op jit(solution)/shard_map/apply/pallas_call | solution.py:113
  49.7 0.4 collective-permute-start.6
  50.2 1.0 %collective-permute-done.6.pair_ref = f32[64,512]{1,0:T(8,128)S(1)} collective-permute-done((f32[64,512]{1,0:T(8,128)S(1)}, f32[64,512]{1,0:T(8,128)S(1)}, u32[]{:S(2)}, u32[]{:S(2)}) %collective-permute-start.6) | collective-permute-done | bytes 131104 | tf_op jit(solution)/shard_map/ppermute | solution.py:147
  51.2 1.9 %collective-permute-start.7 = (f32[128,512]{1,0:T(8,128)S(1)}, f32[128,512]{1,0:T(8,128)S(1)}, u32[]{:S(2)}, u32[]{:S(2)}) collective-permute-start(f32[128,512]{1,0:T(8,128)S(1)} %pad_maximum_fusion.2), channel_id=1, source_target_pairs={{1,2},{2,1},{3,4},{4,3},{5,6},{6,5},{7,8},{8,7},{9,10},{10,9},{11,... | collective-permute-start | bytes 786440 | tf_op jit(solution)/shard_map/ppermute | solution.py:148
  53.1 8.4 %collective-permute-done.7.far_ref = f32[128,512]{1,0:T(8,128)S(1)} collective-permute-done((f32[128,512]{1,0:T(8,128)S(1)}, f32[128,512]{1,0:T(8,128)S(1)}, u32[]{:S(2)}, u32[]{:S(2)}) %collective-permute-start.7) | collective-permute-done | bytes 262176 | tf_op jit(solution)/shard_map/ppermute | solution.py:148
  61.5 5.1 %collective-permute-start.8 = (f32[64,512]{1,0:T(8,128)S(1)}, f32[64,512]{1,0:T(8,128)S(1)}, u32[]{:S(2)}, u32[]{:S(2)}) collective-permute-start(f32[64,512]{1,0:T(8,128)S(1)} %slice.13), channel_id=1, source_target_pairs={{0,1},{1,0},{2,3},{3,2},{4,5},{5,4},{6,7},{7,6},{8,9},{9,8},{10,11... | collective-permute-start | bytes 393224 | tf_op jit(solution)/shard_map/ppermute | solution.py:151
  66.6 1.0 %collective-permute-done.8.cross_ref = f32[64,512]{1,0:T(8,128)S(1)} collective-permute-done((f32[64,512]{1,0:T(8,128)S(1)}, f32[64,512]{1,0:T(8,128)S(1)}, u32[]{:S(2)}, u32[]{:S(2)}) %collective-permute-start.8) | collective-permute-done | bytes 131104 | tf_op jit(solution)/shard_map/ppermute | solution.py:151
  67.5 2.2 %apply.5 = f32[64,512]{1,0:T(8,128)} custom-call(bf16[512,2304]{1,0:T(8,128)(2,1)S(1)} %get-tuple-element.12.high_ref, bf16[512,2304]{1,0:T(8,128)(2,1)S(1)} %get-tuple-element.13.low_ref, f32[64,512]{1,0:T(8,128)S(1)} %copy-done, f32[64,512]{1,0:T(8,128)S(1)} %apply.4.own_ref, f32[64,512]{1,0:T(8,128)S(1)} %collective-permute-done.6.pair_ref, ...), custom_call_target="tpu_custom_call" | custom-call | flops 452984832 | bytes 4718592 | tf_op jit(solution)/shard_map/apply/pallas_call | solution.py:113
  (5 shorter events, 0.1 us)
Async XLA Ops:
  0.0 9.9 %collective-permute-start = (f32[64,512]{1,0:T(8,128)}, f32[64,512]{1,0:T(8,128)S(1)}, u32[]{:S(2)}, u32[]{:S(2)}) collective-permute-start(f32[64,512]{1,0:T(8,128)} %seeds_ref.5), channel_id=1, source_target_pairs={{0,1},{1,0},{2,3},{3,2},{4,5},{5,4},{6,7},{7,6},{8,9},{9,8},{10,11... | collective-permute-start | bytes 393224 | tf_op jit(solution)/shard_map/ppermute | solution.py:147
  2.2 15.8 %all-to-all-start = ((f32[8,8,512]{2,0,1:T(8,128)}), f32[8,8,512]{2,0,1:T(8,128)S(1)}, u32[]{:S(2)}, u32[]{:S(2)}) async-start(f32[8,8,512]{2,0,1:T(8,128)} %bitcast.5), calls=%async_computation | async-start | bytes 262144 | tf_op jit(solution)/shard_map/all_to_all | solution.py:143
  10.8 10.7 %collective-permute-start.1 = (f32[128,512]{1,0:T(8,128)S(1)}, f32[128,512]{1,0:T(8,128)S(1)}, u32[]{:S(2)}, u32[]{:S(2)}) collective-permute-start(f32[128,512]{1,0:T(8,128)S(1)} %pad_maximum_fusion), channel_id=1, source_target_pairs={{1,2},{2,1},{3,4},{4,3},{5,6},{6,5},{7,8},{8,7},{9,10},{10,9},{11,... | collective-permute-start | bytes 786440 | tf_op jit(solution)/shard_map/ppermute | solution.py:148
  18.0 10.2 %copy-start = (f32[64,512]{1,0:T(8,128)S(1)}, f32[64,512]{1,0:T(8,128)}, u32[]{:S(2)}) copy-start(f32[64,512]{1,0:T(8,128)} %seeds_ref.5) | copy-start | bytes 393220
  21.6 6.6 %collective-permute-start.2 = (f32[64,512]{1,0:T(8,128)S(1)}, f32[64,512]{1,0:T(8,128)S(1)}, u32[]{:S(2)}, u32[]{:S(2)}) collective-permute-start(f32[64,512]{1,0:T(8,128)S(1)} %slice.9), channel_id=1, source_target_pairs={{0,1},{1,0},{2,3},{3,2},{4,5},{5,4},{6,7},{7,6},{8,9},{9,8},{10,11... | collective-permute-start | bytes 393224 | tf_op jit(solution)/shard_map/ppermute | solution.py:151
  29.8 1.4 %collective-permute-start.3 = (f32[64,512]{1,0:T(8,128)S(1)}, f32[64,512]{1,0:T(8,128)S(1)}, u32[]{:S(2)}, u32[]{:S(2)}) collective-permute-start(f32[64,512]{1,0:T(8,128)S(1)} %apply.3.own_ref), channel_id=1, source_target_pairs={{0,1},{1,0},{2,3},{3,2},{4,5},{5,4},{6,7},{7,6},{8,9},{9,8},{10,11... | collective-permute-start | bytes 393224 | tf_op jit(solution)/shard_map/ppermute | solution.py:147
  31.3 11.3 %collective-permute-start.4 = (f32[128,512]{1,0:T(8,128)S(1)}, f32[128,512]{1,0:T(8,128)S(1)}, u32[]{:S(2)}, u32[]{:S(2)}) collective-permute-start(f32[128,512]{1,0:T(8,128)S(1)} %pad_maximum_fusion.1), channel_id=1, source_target_pairs={{1,2},{2,1},{3,4},{4,3},{5,6},{6,5},{7,8},{8,7},{9,10},{10,9},{11,... | collective-permute-start | bytes 786440 | tf_op jit(solution)/shard_map/ppermute | solution.py:148
  42.6 5.5 %collective-permute-start.5 = (f32[64,512]{1,0:T(8,128)S(1)}, f32[64,512]{1,0:T(8,128)S(1)}, u32[]{:S(2)}, u32[]{:S(2)}) collective-permute-start(f32[64,512]{1,0:T(8,128)S(1)} %slice.12), channel_id=1, source_target_pairs={{0,1},{1,0},{2,3},{3,2},{4,5},{5,4},{6,7},{7,6},{8,9},{9,8},{10,11... | collective-permute-start | bytes 393224 | tf_op jit(solution)/shard_map/ppermute | solution.py:151
  49.7 1.4 %collective-permute-start.6 = (f32[64,512]{1,0:T(8,128)S(1)}, f32[64,512]{1,0:T(8,128)S(1)}, u32[]{:S(2)}, u32[]{:S(2)}) collective-permute-start(f32[64,512]{1,0:T(8,128)S(1)} %apply.4.own_ref), channel_id=1, source_target_pairs={{0,1},{1,0},{2,3},{3,2},{4,5},{5,4},{6,7},{7,6},{8,9},{9,8},{10,11... | collective-permute-start | bytes 393224 | tf_op jit(solution)/shard_map/ppermute | solution.py:147
  51.2 10.3 %collective-permute-start.7 = (f32[128,512]{1,0:T(8,128)S(1)}, f32[128,512]{1,0:T(8,128)S(1)}, u32[]{:S(2)}, u32[]{:S(2)}) collective-permute-start(f32[128,512]{1,0:T(8,128)S(1)} %pad_maximum_fusion.2), channel_id=1, source_target_pairs={{1,2},{2,1},{3,4},{4,3},{5,6},{6,5},{7,8},{8,7},{9,10},{10,9},{11,... | collective-permute-start | bytes 786440 | tf_op jit(solution)/shard_map/ppermute | solution.py:148
  61.5 6.1 %collective-permute-start.8 = (f32[64,512]{1,0:T(8,128)S(1)}, f32[64,512]{1,0:T(8,128)S(1)}, u32[]{:S(2)}, u32[]{:S(2)}) collective-permute-start(f32[64,512]{1,0:T(8,128)S(1)} %slice.13), channel_id=1, source_target_pairs={{0,1},{1,0},{2,3},{3,2},{4,5},{5,4},{6,7},{7,6},{8,9},{9,8},{10,11... | collective-permute-start | bytes 393224 | tf_op jit(solution)/shard_map/ppermute | solution.py:151

commit v4 on v3

--- a/solution.py
+++ b/solution.py
@@ -90,15 +90,30 @@
     )(edges)
 
 
-def apply_kernel(high_ref, low_ref, seeds_ref, own_ref, pair_ref, far_ref, cross_ref, out_ref, window_ref):
+def apply_kernel(high_ref, low_ref, seeds_ref, *refs, places, count):
+    *panel_refs, out_ref, window_ref = refs
     channels, events = out_ref.shape
-    second = lax.axis_index("cols") % 2
-    blocks = [own_ref[...], pair_ref[...], cross_ref[...], far_ref[:channels], far_ref[channels:]]
-    for value, place in zip(blocks, (2, 3, 4, 1, 0)):
+    device = lax.axis_index("rows") * lax.axis_size("cols") + lax.axis_index("cols")
+    second = device % 2
+    blocks = [ref[at:at + channels] for ref in panel_refs for at in range(0, ref.shape[0], channels)]
+    for value, place in zip(blocks, places):
         at = pl.multiple_of((place + second * (4 - 2 * place)) * events, events)
         high = value.astype(jnp.bfloat16)
         window_ref[:channels, pl.ds(at, events)] = high
         window_ref[channels:, pl.ds(at, events)] = (value - high.astype(jnp.float32)).astype(jnp.bfloat16)
+
+    def clear(at, width):
+        window_ref[:, pl.ds(pl.multiple_of(at, events), width)] = jnp.zeros((2 * channels, width), jnp.bfloat16)
+
+    for edge in range(2):
+        @pl.when(device == edge)
+        def _():
+            clear(0, (2 - edge) * events)
+
+        @pl.when(device == count - 1 - edge)
+        def _():
+            clear((3 + edge) * events, (2 - edge) * events)
+
     for part in range(events // BLOCK):
         rows = slice(part * BLOCK, (part + 1) * BLOCK)
         window = window_ref[:, part * BLOCK:part * BLOCK + SPAN]
@@ -108,10 +123,10 @@
         out_ref[:, rows] = 0.9 * total + 0.1 * seeds_ref[:, rows]
 
 
-def apply(matrix, seeds, panels):
+def apply(matrix, seeds, panels, places, count):
     channels, events = seeds.shape
     return pl.pallas_call(
-        apply_kernel,
+        functools.partial(apply_kernel, places=places, count=count),
         out_shape=jax.ShapeDtypeStruct(seeds.shape, jnp.float32),
         scratch_shapes=[pltpu.VMEM((2 * channels, 5 * events), jnp.bfloat16)],
         compiler_params=pltpu.CompilerParams(vmem_limit_bytes=32 * 2**20),
@@ -138,18 +153,19 @@
 def on_device(offsets, weights, seeds, *, count):
     channels = seeds.shape[0]
     on_chip = [(i, i ^ 1) for i in range(count)]
-    off_chip = [(i, i + 1 if i % 2 else i - 1) for i in range(1, count - 1)]
+    ring = lambda step: [(i, (i + step - 2 * step * (i % 2)) % count) for i in range(count)]
     edges = pack(offsets, weights)
     edges = lax.all_to_all(edges, "cols", split_axis=1, concat_axis=0, tiled=True)
     matrix = build(edges)
     scores = seeds
     for step in range(ITERS):
+        near = lax.ppermute(scores, AXES, ring(-1))
         pair = lax.ppermute(scores, AXES, on_chip)
-        far = lax.ppermute(jnp.concatenate([scores, pair], axis=0), AXES, off_chip)
+        away = lax.ppermute(scores, AXES, ring(2))
         if step == 0:
-            far, *matrix = lax.optimization_barrier((far, *matrix))
-        cross = lax.ppermute(far[:channels], AXES, on_chip)
-        scores = apply(matrix, seeds, [scores, pair, far, cross])
+            near, away, *matrix = lax.optimization_barrier((near, away, *matrix))
+        cross = lax.ppermute(near, AXES, on_chip)
+        scores = apply(matrix, seeds, [scores, pair, near, away, cross], (2, 3, 1, 0, 4), count)
     return scores
 
 

time: 70.1 us -> 65.8 us (0.939)
  waiting for transfers between devices: 25.5 us -> 6.65 us
  starting transfers between devices: 32.8 us -> 48 us
  other arithmetic: 0.96 us -> 0 us
    ppermute x6 -> x9, starting transfers between devices: 23.5 us -> 39.7 us  [the longest x3 32.2 us: on_device(): away = lax.ppermute(scores, AXES, ring(2))]
    ppermute x6 -> x9, waiting for transfers between devices: 20.7 us -> 6.64 us  [the longest x3 3.47 us: on_device(): near = lax.ppermute(scores, AXES, ring(-1))]
    all_to_all x1, waiting for transfers between devices: 2.76 us -> 0.01 us  [on_device(): lax.all_to_all(edges, 'cols', split_axis=1, concat_axis=0, tiled=True)]
    ppermute x3, waiting for transfers between devices: 1.98 us -> 0.01 us  [on_device(): pair = lax.ppermute(scores, AXES, on_chip)]
    ppermute x3, starting transfers between devices: 1.57 us -> 0.01 us  [on_device(): pair = lax.ppermute(scores, AXES, on_chip)]
    concatenate x3 -> x0, other arithmetic: 0.96 us -> none  [on_device(): far = lax.ppermute(jnp.concatenate([scores, pair], axis=0), AXES, off_chip)]
  transfers between devices with their start and end apart: 10 -> 13, of which waited for: 8 -> 4; matrix products, arithmetic and copies ran while one was open for 1% -> 0% of each run, Pallas kernels for 7% -> 5%
where the time goes in v4:
time: 65.8 us; the launch traced here: 65.3 us
  starting transfers between devices  48 us (73%)
  Pallas kernels  10.7 us (16%)
  waiting for transfers between devices  6.65 us (10%)
    ppermute x3, starting transfers between devices, on_device(): away = lax.ppermute(scores, AXES, ring(2))  32.2 us
    all_to_all x1, starting transfers between devices, on_device(): lax.all_to_all(edges, 'cols', split_axis=1, concat_axis=0, tiled=True)  8.24 us
    ppermute x3, starting transfers between devices, on_device(): cross = lax.ppermute(near, AXES, on_chip)  7.37 us
    pallas_call x3, Pallas kernels, apply(): pl.pallas_call(functools.partial(apply_kernel, places=places, count=count...  5.63 us
    pallas_call x1, Pallas kernels, build(): pl.pallas_call(build_kernel, out_shape=(out, out), scratch_shapes=[pltpu....  3.49 us
    ppermute x3, waiting for transfers between devices, on_device(): near = lax.ppermute(scores, AXES, ring(-1))  3.47 us
    ppermute x3, waiting for transfers between devices, on_device(): cross = lax.ppermute(near, AXES, on_chip)  3.17 us
    pallas_call x1, Pallas kernels, pack(): pl.pallas_call(pack_kernel, out_shape=jax.ShapeDtypeStruct((2 * slots, ev...  1.54 us
  transfers between devices with their start and end apart: 13, of which 4 were waited for; matrix products, arithmetic and copies ran while one was open for 0% of the time, Pallas kernels for 5%

profile of v4, /device:TPU:33, one launch (start us, length us, event | category | flops | bytes accessed | tf_op | source)
XLA Modules:
  0.0 65.3 jit_solution(6487340625290055860)
XLA Ops:
  0.0 1.5 %pack.1 = f32[8,4096]{1,0:T(8,128)} custom-call(s32[4,4096]{1,0:T(4,128)} %offsets_ref.1, f32[4,4096]{1,0:T(4,128)} %weights_ref.1), custom_call_target="tpu_custom_call" | custom-call | tf_op jit(solution)/shard_map/pack/pallas_call | solution.py:146
  1.5 8.2 %all-to-all-start = ((f32[8,8,512]{2,0,1:T(8,128)}), f32[8,8,512]{2,0,1:T(8,128)S(1)}, u32[]{:S(2)}, u32[]{:S(2)}) async-start(f32[8,8,512]{2,0,1:T(8,128)} %bitcast.5), calls=%async_computation | async-start | bytes 262144 | tf_op jit(solution)/shard_map/all_to_all | solution.py:158
  9.8 0.0 collective-permute-start.2
  9.8 8.9 %collective-permute-start.1 = (f32[64,512]{1,0:T(8,128)}, f32[64,512]{1,0:T(8,128)S(1)}, u32[]{:S(2)}, u32[]{:S(2)}) collective-permute-start(f32[64,512]{1,0:T(8,128)} %seeds_ref.5), channel_id=1, source_target_pairs={{0,2},{1,255},{2,4},{3,1},{4,6},{5,3},{6,8},{7,5},{8,10},{9,7},{10... | collective-permute-start | bytes 393224 | tf_op jit(solution)/shard_map/ppermute | solution.py:164
  18.7 0.0 collective-permute-start
  18.7 0.0 all-to-all-done
  18.7 3.5 %build.1 = (bf16[512,2304]{1,0:T(8,128)(2,1)S(1)}, bf16[512,2304]{1,0:T(8,128)(2,1)S(1)}) custom-call(f32[64,512]{1,0:T(8,128)S(1)} %bitcast.4), custom_call_target="tpu_custom_call" | custom-call | flops 3000000000 | bytes 4718592 | tf_op jit(solution)/shard_map/build/pallas_call | solution.py:83
  22.2 0.0 collective-permute-done.1.refs_3_
  22.2 3.5 %collective-permute-done.refs_2_ = f32[64,512]{1,0:T(8,128)S(1)} collective-permute-done((f32[64,512]{1,0:T(8,128)}, f32[64,512]{1,0:T(8,128)S(1)}, u32[]{:S(2)}, u32[]{:S(2)}) %collective-permute-start) | collective-permute-done | bytes 131104 | tf_op jit(solution)/shard_map/ppermute | solution.py:162
  25.7 0.1 collective-permute-start.3
  25.8 0.0 collective-permute-done.2.refs_1_
  25.9 1.2 %collective-permute-done.3.refs_4_ = f32[64,512]{1,0:T(8,128)S(1)} collective-permute-done((f32[64,512]{1,0:T(8,128)S(1)}, f32[64,512]{1,0:T(8,128)S(1)}, u32[]{:S(2)}, u32[]{:S(2)}) %collective-permute-start.3) | collective-permute-done | bytes 131104 | tf_op jit(solution)/shard_map/ppermute | solution.py:167
  27.1 0.0 copy-done
  27.1 1.7 %apply.3.refs_0_ = f32[64,512]{1,0:T(8,128)S(1)} custom-call(bf16[512,2304]{1,0:T(8,128)(2,1)S(1)} %get-tuple-element.13.high_ref, bf16[512,2304]{1,0:T(8,128)(2,1)S(1)} %get-tuple-element.14.low_ref, f32[64,512]{1,0:T(8,128)S(1)} %copy-done, f32[64,512]{1,0:T(8,128)S(1)} %copy-done, f32[64,512]{1,0:T(8,128)S(1)} %collective-permute-done.2.refs_1_, ...), custom_call_target="tpu_custom_call" | custom-call | flops 452984832 | bytes 4718592 | tf_op jit(solution)/shard_map/apply/pallas_call | solution.py:128
  28.7 0.1 collective-permute-start.5
  28.8 8.7 %collective-permute-start.6 = (f32[64,512]{1,0:T(8,128)S(1)}, f32[64,512]{1,0:T(8,128)S(1)}, u32[]{:S(2)}, u32[]{:S(2)}) collective-permute-start(f32[64,512]{1,0:T(8,128)S(1)} %apply.3.refs_0_), channel_id=1, source_target_pairs={{0,2},{1,255},{2,4},{3,1},{4,6},{5,3},{6,8},{7,5},{8,10},{9,7},{10... | collective-permute-start | bytes 393224 | tf_op jit(solution)/shard_map/ppermute | solution.py:164
  37.5 0.0 collective-permute-start.4
  37.5 0.0 collective-permute-done.5.refs_2_
  37.5 4.1 %collective-permute-start.7 = (f32[64,512]{1,0:T(8,128)S(1)}, f32[64,512]{1,0:T(8,128)S(1)}, u32[]{:S(2)}, u32[]{:S(2)}) collective-permute-start(f32[64,512]{1,0:T(8,128)S(1)} %collective-permute-done.5.refs_2_), channel_id=1, source_target_pairs={{0,1},{1,0},{2,3},{3,2},{4,5},{5,4},{6,7},{7,6},{8,9},{9,8},{10,11... | collective-permute-start | bytes 393224 | tf_op jit(solution)/shard_map/ppermute | solution.py:167
  41.6 0.0 collective-permute-done.6.refs_3_
  41.6 0.0 collective-permute-done.4.refs_1_
  41.7 1.0 %collective-permute-done.7.refs_4_ = f32[64,512]{1,0:T(8,128)S(1)} collective-permute-done((f32[64,512]{1,0:T(8,128)S(1)}, f32[64,512]{1,0:T(8,128)S(1)}, u32[]{:S(2)}, u32[]{:S(2)}) %collective-permute-start.7) | collective-permute-done | bytes 131104 | tf_op jit(solution)/shard_map/ppermute | solution.py:167
  42.6 1.6 %apply.4.refs_0_ = f32[64,512]{1,0:T(8,128)S(1)} custom-call(bf16[512,2304]{1,0:T(8,128)(2,1)S(1)} %get-tuple-element.13.high_ref, bf16[512,2304]{1,0:T(8,128)(2,1)S(1)} %get-tuple-element.14.low_ref, f32[64,512]{1,0:T(8,128)S(1)} %copy-done, f32[64,512]{1,0:T(8,128)S(1)} %apply.3.refs_0_, f32[64,512]{1,0:T(8,128)S(1)} %collective-permute-done.4.refs_1_, ...), custom_call_target="tpu_custom_call" | custom-call | flops 452984832 | bytes 4718592 | tf_op jit(solution)/shard_map/apply/pallas_call | solution.py:128
  44.3 0.1 collective-permute-start.9
  44.4 14.5 %collective-permute-start.10 = (f32[64,512]{1,0:T(8,128)S(1)}, f32[64,512]{1,0:T(8,128)S(1)}, u32[]{:S(2)}, u32[]{:S(2)}) collective-permute-start(f32[64,512]{1,0:T(8,128)S(1)} %apply.4.refs_0_), channel_id=1, source_target_pairs={{0,2},{1,255},{2,4},{3,1},{4,6},{5,3},{6,8},{7,5},{8,10},{9,7},{10... | collective-permute-start | bytes 393224 | tf_op jit(solution)/shard_map/ppermute | solution.py:164
  58.9 0.0 collective-permute-start.8
  58.9 0.0 collective-permute-done.9.refs_2_
  58.9 3.1 %collective-permute-start.11 = (f32[64,512]{1,0:T(8,128)S(1)}, f32[64,512]{1,0:T(8,128)S(1)}, u32[]{:S(2)}, u32[]{:S(2)}) collective-permute-start(f32[64,512]{1,0:T(8,128)S(1)} %collective-permute-done.9.refs_2_), channel_id=1, source_target_pairs={{0,1},{1,0},{2,3},{3,2},{4,5},{5,4},{6,7},{7,6},{8,9},{9,8},{10,11... | collective-permute-start | bytes 393224 | tf_op jit(solution)/shard_map/ppermute | solution.py:167
  62.0 0.0 collective-permute-done.10.refs_3_
  62.0 0.0 collective-permute-done.8.refs_1_
  62.0 1.0 %collective-permute-done.11.refs_4_ = f32[64,512]{1,0:T(8,128)S(1)} collective-permute-done((f32[64,512]{1,0:T(8,128)S(1)}, f32[64,512]{1,0:T(8,128)S(1)}, u32[]{:S(2)}, u32[]{:S(2)}) %collective-permute-start.11) | collective-permute-done | bytes 131104 | tf_op jit(solution)/shard_map/ppermute | solution.py:167
  63.0 2.3 %apply.5 = f32[64,512]{1,0:T(8,128)} custom-call(bf16[512,2304]{1,0:T(8,128)(2,1)S(1)} %get-tuple-element.13.high_ref, bf16[512,2304]{1,0:T(8,128)(2,1)S(1)} %get-tuple-element.14.low_ref, f32[64,512]{1,0:T(8,128)S(1)} %copy-done, f32[64,512]{1,0:T(8,128)S(1)} %apply.4.refs_0_, f32[64,512]{1,0:T(8,128)S(1)} %collective-permute-done.8.refs_1_, ...), custom_call_target="tpu_custom_call" | custom-call | flops 452984832 | bytes 4718592 | tf_op jit(solution)/shard_map/apply/pallas_call | solution.py:128
  (1 shorter events, 0.0 us)
Async XLA Ops:
  1.5 17.2 %all-to-all-start = ((f32[8,8,512]{2,0,1:T(8,128)}), f32[8,8,512]{2,0,1:T(8,128)S(1)}, u32[]{:S(2)}, u32[]{:S(2)}) async-start(f32[8,8,512]{2,0,1:T(8,128)} %bitcast.5), calls=%async_computation | async-start | bytes 262144 | tf_op jit(solution)/shard_map/all_to_all | solution.py:158
  9.8 16.1 %collective-permute-start.2 = (f32[64,512]{1,0:T(8,128)}, f32[64,512]{1,0:T(8,128)S(1)}, u32[]{:S(2)}, u32[]{:S(2)}) collective-permute-start(f32[64,512]{1,0:T(8,128)} %seeds_ref.5), channel_id=1, source_target_pairs={{0,1},{1,0},{2,3},{3,2},{4,5},{5,4},{6,7},{7,6},{8,9},{9,8},{10,11... | collective-permute-start | bytes 393224 | tf_op jit(solution)/shard_map/ppermute | solution.py:163
  9.8 12.5 %collective-permute-start.1 = (f32[64,512]{1,0:T(8,128)}, f32[64,512]{1,0:T(8,128)S(1)}, u32[]{:S(2)}, u32[]{:S(2)}) collective-permute-start(f32[64,512]{1,0:T(8,128)} %seeds_ref.5), channel_id=1, source_target_pairs={{0,2},{1,255},{2,4},{3,1},{4,6},{5,3},{6,8},{7,5},{8,10},{9,7},{10... | collective-permute-start | bytes 393224 | tf_op jit(solution)/shard_map/ppermute | solution.py:164
  18.7 7.0 %collective-permute-start = (f32[64,512]{1,0:T(8,128)}, f32[64,512]{1,0:T(8,128)S(1)}, u32[]{:S(2)}, u32[]{:S(2)}) collective-permute-start(f32[64,512]{1,0:T(8,128)} %seeds_ref.5), channel_id=1, source_target_pairs={{0,255},{1,2},{2,1},{3,4},{4,3},{5,6},{6,5},{7,8},{8,7},{9,10},{10... | collective-permute-start | bytes 393224 | tf_op jit(solution)/shard_map/ppermute | solution.py:162
  18.7 8.3 %copy-start = (f32[64,512]{1,0:T(8,128)S(1)}, f32[64,512]{1,0:T(8,128)}, u32[]{:S(2)}) copy-start(f32[64,512]{1,0:T(8,128)} %seeds_ref.5) | copy-start | bytes 393220
  25.7 1.3 %collective-permute-start.3 = (f32[64,512]{1,0:T(8,128)S(1)}, f32[64,512]{1,0:T(8,128)S(1)}, u32[]{:S(2)}, u32[]{:S(2)}) collective-permute-start(f32[64,512]{1,0:T(8,128)S(1)} %collective-permute-done.refs_2_), channel_id=1, source_target_pairs={{0,1},{1,0},{2,3},{3,2},{4,5},{5,4},{6,7},{7,6},{8,9},{9,8},{10,11... | collective-permute-start | bytes 393224 | tf_op jit(solution)/shard_map/ppermute | solution.py:167
  28.7 8.8 %collective-permute-start.5 = (f32[64,512]{1,0:T(8,128)S(1)}, f32[64,512]{1,0:T(8,128)S(1)}, u32[]{:S(2)}, u32[]{:S(2)}) collective-permute-start(f32[64,512]{1,0:T(8,128)S(1)} %apply.3.refs_0_), channel_id=1, source_target_pairs={{0,255},{1,2},{2,1},{3,4},{4,3},{5,6},{6,5},{7,8},{8,7},{9,10},{10... | collective-permute-start | bytes 393224 | tf_op jit(solution)/shard_map/ppermute | solution.py:162
  28.8 12.8 %collective-permute-start.6 = (f32[64,512]{1,0:T(8,128)S(1)}, f32[64,512]{1,0:T(8,128)S(1)}, u32[]{:S(2)}, u32[]{:S(2)}) collective-permute-start(f32[64,512]{1,0:T(8,128)S(1)} %apply.3.refs_0_), channel_id=1, source_target_pairs={{0,2},{1,255},{2,4},{3,1},{4,6},{5,3},{6,8},{7,5},{8,10},{9,7},{10... | collective-permute-start | bytes 393224 | tf_op jit(solution)/shard_map/ppermute | solution.py:164
  37.5 4.1 %collective-permute-start.4 = (f32[64,512]{1,0:T(8,128)S(1)}, f32[64,512]{1,0:T(8,128)S(1)}, u32[]{:S(2)}, u32[]{:S(2)}) collective-permute-start(f32[64,512]{1,0:T(8,128)S(1)} %apply.3.refs_0_), channel_id=1, source_target_pairs={{0,1},{1,0},{2,3},{3,2},{4,5},{5,4},{6,7},{7,6},{8,9},{9,8},{10,11... | collective-permute-start | bytes 393224 | tf_op jit(solution)/shard_map/ppermute | solution.py:163
  37.5 5.1 %collective-permute-start.7 = (f32[64,512]{1,0:T(8,128)S(1)}, f32[64,512]{1,0:T(8,128)S(1)}, u32[]{:S(2)}, u32[]{:S(2)}) collective-permute-start(f32[64,512]{1,0:T(8,128)S(1)} %collective-permute-done.5.refs_2_), channel_id=1, source_target_pairs={{0,1},{1,0},{2,3},{3,2},{4,5},{5,4},{6,7},{7,6},{8,9},{9,8},{10,11... | collective-permute-start | bytes 393224 | tf_op jit(solution)/shard_map/ppermute | solution.py:167
  44.3 14.6 %collective-permute-start.9 = (f32[64,512]{1,0:T(8,128)S(1)}, f32[64,512]{1,0:T(8,128)S(1)}, u32[]{:S(2)}, u32[]{:S(2)}) collective-permute-start(f32[64,512]{1,0:T(8,128)S(1)} %apply.4.refs_0_), channel_id=1, source_target_pairs={{0,255},{1,2},{2,1},{3,4},{4,3},{5,6},{6,5},{7,8},{8,7},{9,10},{10... | collective-permute-start | bytes 393224 | tf_op jit(solution)/shard_map/ppermute | solution.py:162
  44.4 17.6 %collective-permute-start.10 = (f32[64,512]{1,0:T(8,128)S(1)}, f32[64,512]{1,0:T(8,128)S(1)}, u32[]{:S(2)}, u32[]{:S(2)}) collective-permute-start(f32[64,512]{1,0:T(8,128)S(1)} %apply.4.refs_0_), channel_id=1, source_target_pairs={{0,2},{1,255},{2,4},{3,1},{4,6},{5,3},{6,8},{7,5},{8,10},{9,7},{10... | collective-permute-start | bytes 393224 | tf_op jit(solution)/shard_map/ppermute | solution.py:164
  58.9 3.1 %collective-permute-start.8 = (f32[64,512]{1,0:T(8,128)S(1)}, f32[64,512]{1,0:T(8,128)S(1)}, u32[]{:S(2)}, u32[]{:S(2)}) collective-permute-start(f32[64,512]{1,0:T(8,128)S(1)} %apply.4.refs_0_), channel_id=1, source_target_pairs={{0,1},{1,0},{2,3},{3,2},{4,5},{5,4},{6,7},{7,6},{8,9},{9,8},{10,11... | collective-permute-start | bytes 393224 | tf_op jit(solution)/shard_map/ppermute | solution.py:163
  58.9 4.1 %collective-permute-start.11 = (f32[64,512]{1,0:T(8,128)S(1)}, f32[64,512]{1,0:T(8,128)S(1)}, u32[]{:S(2)}, u32[]{:S(2)}) collective-permute-start(f32[64,512]{1,0:T(8,128)S(1)} %collective-permute-done.9.refs_2_), channel_id=1, source_target_pairs={{0,1},{1,0},{2,3},{3,2},{4,5},{5,4},{6,7},{7,6},{8,9},{9,8},{10,11... | collective-permute-start | bytes 393224 | tf_op jit(solution)/shard_map/ppermute | solution.py:167

commit v5 on v4

--- a/solution.py
+++ b/solution.py
@@ -90,17 +90,41 @@
     )(edges)
 
 
-def apply_kernel(high_ref, low_ref, seeds_ref, *refs, places, count):
+def split(ref, at, value):
+    channels, events = value.shape
+    at = pl.multiple_of(at, events)
+    high = value.astype(jnp.bfloat16)
+    ref[:channels, pl.ds(at, events)] = high
+    ref[channels:, pl.ds(at, events)] = (value - high.astype(jnp.float32)).astype(jnp.bfloat16)
+
+
+def product(window, high, low):
+    channels = window.shape[0] // 2
+    both = lax.dot_general(window, high, NT, preferred_element_type=jnp.float32)
+    rest = lax.dot_general(window[:channels], low, NT, preferred_element_type=jnp.float32)
+    return both[:channels] + (both[channels:] + rest)
+
+
+def chip_kernel(high_ref, low_ref, seeds_ref, own_ref, pair_ref, out_ref, window_ref):
+    events = out_ref.shape[1]
+    second = lax.axis_index("cols") % 2
+    split(window_ref, second * events, own_ref[...])
+    split(window_ref, (1 - second) * events, pair_ref[...])
+    for part in range(events // BLOCK):
+        rows = slice(part * BLOCK, (part + 1) * BLOCK)
+        columns = pl.ds(pl.multiple_of((2 - second) * events - part * BLOCK, BLOCK), 2 * events)
+        total = product(window_ref[...], high_ref[rows, columns], low_ref[rows, columns])
+        out_ref[:, rows] = 0.9 * total + 0.1 * seeds_ref[:, rows]
+
+
+def far_kernel(high_ref, low_ref, part_ref, *refs, places, count):
     *panel_refs, out_ref, window_ref = refs
     channels, events = out_ref.shape
     device = lax.axis_index("rows") * lax.axis_size("cols") + lax.axis_index("cols")
     second = device % 2
     blocks = [ref[at:at + channels] for ref in panel_refs for at in range(0, ref.shape[0], channels)]
     for value, place in zip(blocks, places):
-        at = pl.multiple_of((place + second * (4 - 2 * place)) * events, events)
-        high = value.astype(jnp.bfloat16)
-        window_ref[:channels, pl.ds(at, events)] = high
-        window_ref[channels:, pl.ds(at, events)] = (value - high.astype(jnp.float32)).astype(jnp.bfloat16)
+        split(window_ref, (place + second * (4 - 2 * place)) * events, value)
 
     def clear(at, width):
         window_ref[:, pl.ds(pl.multiple_of(at, events), width)] = jnp.zeros((2 * channels, width), jnp.bfloat16)
@@ -114,25 +138,38 @@
         def _():
             clear((3 + edge) * events, (2 - edge) * events)
 
-    for part in range(events // BLOCK):
-        rows = slice(part * BLOCK, (part + 1) * BLOCK)
-        window = window_ref[:, part * BLOCK:part * BLOCK + SPAN]
-        both = lax.dot_general(window, high_ref[rows], NT, preferred_element_type=jnp.float32)
-        rest = lax.dot_general(window[:channels], low_ref[rows], NT, preferred_element_type=jnp.float32)
-        total = both[:channels] + (both[channels:] + rest)
-        out_ref[:, rows] = 0.9 * total + 0.1 * seeds_ref[:, rows]
-
-
-def apply(matrix, seeds, panels, places, count):
+    for core in range(2):
+        @pl.when(second == core)
+        def _():
+            here = (2 - core) * events
+            for part in range(events // BLOCK):
+                rows = slice(part * BLOCK, (part + 1) * BLOCK)
+                total = part_ref[:, rows]
+                for first, last in ((part * BLOCK, here), (here + 2 * events, part * BLOCK + SPAN)):
+                    columns = slice(first - part * BLOCK, last - part * BLOCK)
+                    total += 0.9 * product(window_ref[:, first:last], high_ref[rows, columns], low_ref[rows, columns])
+                out_ref[:, rows] = total
+
+
+def call(kernel, name, seeds, width, *args):
     channels, events = seeds.shape
     return pl.pallas_call(
-        functools.partial(apply_kernel, places=places, count=count),
+        kernel,
         out_shape=jax.ShapeDtypeStruct(seeds.shape, jnp.float32),
-        scratch_shapes=[pltpu.VMEM((2 * channels, 5 * events), jnp.bfloat16)],
+        scratch_shapes=[pltpu.VMEM((2 * channels, width * events), jnp.bfloat16)],
         compiler_params=pltpu.CompilerParams(vmem_limit_bytes=32 * 2**20),
-        cost_estimate=pl.CostEstimate(flops=6 * channels * events * SPAN, bytes_accessed=4 * events * SPAN, transcendentals=0),
-        name="apply",
-    )(*matrix, seeds, *panels)
+        cost_estimate=pl.CostEstimate(flops=3 * channels * events * SPAN, bytes_accessed=2 * events * SPAN, transcendentals=0),
+        name=name,
+    )(*args)
+
+
+def chip_part(matrix, seeds, own, pair):
+    return call(chip_kernel, "chip_part", seeds, 2, *matrix, seeds, own, pair)
+
+
+def far_part(matrix, seeds, part, panels, places, count):
+    kernel = functools.partial(far_kernel, places=places, count=count)
+    return call(kernel, "far_part", seeds, 5, *matrix, part, *panels)
 
 
 def pack_kernel(offsets_ref, weights_ref, out_ref):
@@ -154,18 +191,24 @@
     channels = seeds.shape[0]
     on_chip = [(i, i ^ 1) for i in range(count)]
     ring = lambda step: [(i, (i + step - 2 * step * (i % 2)) % count) for i in range(count)]
+    skip = [(i, i + 2 - 4 * (i % 2)) for i in range(count) if 0 <= i + 2 - 4 * (i % 2) < count] + [(1, 0), (count - 2, count - 1)]
     edges = pack(offsets, weights)
     edges = lax.all_to_all(edges, "cols", split_axis=1, concat_axis=0, tiled=True)
     matrix = build(edges)
     scores = seeds
     for step in range(ITERS):
+        pair = lax.ppermute(scores, AXES, on_chip)
         near = lax.ppermute(scores, AXES, ring(-1))
-        pair = lax.ppermute(scores, AXES, on_chip)
-        away = lax.ppermute(scores, AXES, ring(2))
+        away = lax.ppermute(scores, AXES, skip if step == 0 else ring(3))
+        part = chip_part(matrix, seeds, scores, pair)
         if step == 0:
-            near, away, *matrix = lax.optimization_barrier((near, away, *matrix))
-        cross = lax.ppermute(near, AXES, on_chip)
-        scores = apply(matrix, seeds, [scores, pair, near, away, cross], (2, 3, 1, 0, 4), count)
+            near, away, part = lax.optimization_barrier((near, away, part))
+            cross = lax.ppermute(near, AXES, on_chip)
+            scores = far_part(matrix, seeds, part, [away, near, cross], (0, 1, 4), count)
+        else:
+            near, away, part = lax.optimization_barrier((near, away, part))
+            cross = lax.ppermute(jnp.concatenate([near, away], axis=0), AXES, on_chip)
+            scores = far_part(matrix, seeds, part, [near, cross], (1, 4, 0), count)
     return scores
 
 

time: 65.8 us -> 63.8 us (0.970)
  starting transfers between devices: 48 us -> 31.8 us
  waiting for transfers between devices: 6.65 us -> 20.7 us
    ppermute x3 -> x5, waiting for transfers between devices: 0.01 us -> 16.8 us  [the longest x3 14.5 us: on_device(): away = lax.ppermute(scores, AXES, skip if step == 0 else ring(3))]
    ppermute x3 -> x5, starting transfers between devices: 32.2 us -> 22.7 us  [the longest x3 21.7 us: on_device(): away = lax.ppermute(scores, AXES, skip if step == 0 else ring(3))]
    ppermute x3 -> x1, starting transfers between devices: 7.37 us -> 0.14 us  [on_device(): cross = lax.ppermute(near, AXES, on_chip)]
    ppermute x3 -> x1, waiting for transfers between devices: 3.17 us -> 1.21 us  [on_device(): cross = lax.ppermute(near, AXES, on_chip)]
    ppermute x3, waiting for transfers between devices: 3.47 us -> 2.64 us  [on_device(): near = lax.ppermute(scores, AXES, ring(-1))]
    ppermute x3, starting transfers between devices: 0.01 us -> 0.69 us  [on_device(): pair = lax.ppermute(scores, AXES, on_chip)]
    pallas_call x3 -> x6, Pallas kernels: 5.63 us -> 6.02 us  [call(): pl.pallas_call(kernel, out_shape=jax.ShapeDtypeStruct(seeds.shape, jnp.fl...]
  transfers between devices with their start and end apart: 13 -> 13, of which waited for: 4 -> 6; matrix products, arithmetic and copies ran while one was open for 0% -> 0% of each run, Pallas kernels for 5% -> 9%
where the time goes in v5:
time: 63.8 us; the launch traced here: 63.6 us
  starting transfers between devices  31.8 us (50%)
  waiting for transfers between devices  20.7 us (32%)
  Pallas kernels  11.1 us (17%)
    ppermute x3, starting transfers between devices, on_device(): away = lax.ppermute(scores, AXES, skip if step == 0 else ring(3))  21.7 us
    ppermute x3, waiting for transfers between devices, on_device(): away = lax.ppermute(scores, AXES, skip if step == 0 else ring(3))  14.5 us
    all_to_all x1, starting transfers between devices, on_device(): lax.all_to_all(edges, 'cols', split_axis=1, concat_axis=0, tiled=True)  8.24 us
    pallas_call x6, Pallas kernels, call(): pl.pallas_call(kernel, out_shape=jax.ShapeDtypeStruct(seeds.shape, jnp.fl...  6.02 us
    pallas_call x1, Pallas kernels, build(): pl.pallas_call(build_kernel, out_shape=(out, out), scratch_shapes=[pltpu....  3.49 us
    ppermute x3, waiting for transfers between devices, on_device(): near = lax.ppermute(scores, AXES, ring(-1))  2.64 us
    ppermute x2, waiting for transfers between devices, on_device(): cross = lax.ppermute(jnp.concatenate([near, away], axis=0), AXES, on_chip)  2.32 us
    pallas_call x1, Pallas kernels, pack(): pl.pallas_call(pack_kernel, out_shape=jax.ShapeDtypeStruct((2 * slots, ev...  1.54 us
  transfers between devices with their start and end apart: 13, of which 6 were waited for; matrix products, arithmetic and copies ran while one was open for 0% of the time, Pallas kernels for 9%

profile of v5, /device:TPU:33, one launch (start us, length us, event | category | flops | bytes accessed | tf_op | source)
XLA Modules:
  0.0 63.6 jit_solution(16586685909622333025)
XLA Ops:
  0.0 1.5 %pack.1 = f32[8,4096]{1,0:T(8,128)} custom-call(s32[4,4096]{1,0:T(4,128)} %offsets_ref.1, f32[4,4096]{1,0:T(4,128)} %weights_ref.1), custom_call_target="tpu_custom_call" | custom-call | tf_op jit(solution)/shard_map/pack/pallas_call | solution.py:183
  1.5 8.2 %all-to-all-start = ((f32[8,8,512]{2,0,1:T(8,128)}), f32[8,8,512]{2,0,1:T(8,128)S(1)}, u32[]{:S(2)}, u32[]{:S(2)}) async-start(f32[8,8,512]{2,0,1:T(8,128)} %bitcast.5), calls=%async_computation | async-start | bytes 262144 | tf_op jit(solution)/shard_map/all_to_all | solution.py:196
  9.8 0.0 collective-permute-start.2
  9.8 8.9 %collective-permute-start.1 = (f32[64,512]{1,0:T(8,128)}, f32[64,512]{1,0:T(8,128)S(1)}, u32[]{:S(2)}, u32[]{:S(2)}) collective-permute-start(f32[64,512]{1,0:T(8,128)} %seeds_ref.5), channel_id=1, source_target_pairs={{0,2},{2,4},{3,1},{4,6},{5,3},{6,8},{7,5},{8,10},{9,7},{10,12},{11... | collective-permute-start | bytes 393224 | tf_op jit(solution)/shard_map/ppermute | solution.py:202
  18.7 0.0 collective-permute-start
  18.7 0.0 all-to-all-done
  18.7 3.5 %build.1 = (bf16[512,2304]{1,0:T(8,128)(2,1)S(1)}, bf16[512,2304]{1,0:T(8,128)(2,1)S(1)}) custom-call(f32[64,512]{1,0:T(8,128)S(1)} %bitcast.4), custom_call_target="tpu_custom_call" | custom-call | flops 3000000000 | bytes 4718592 | tf_op jit(solution)/shard_map/build/pallas_call | solution.py:83
  22.3 0.8 %chip_part.3.part_ref = f32[64,512]{1,0:T(8,128)S(1)} custom-call(bf16[512,2304]{1,0:T(8,128)(2,1)S(1)} %get-tuple-element.16.high_ref, bf16[512,2304]{1,0:T(8,128)(2,1)S(1)} %get-tuple-element.17.low_ref, f32[64,512]{1,0:T(8,128)S(1)} %copy-done, f32[64,512]{1,0:T(8,128)S(1)} %copy-done, f32[64,512]{1,0:T(8,128)S(1)} %collective-permute-done.2.pair_ref), custom_call_target="tpu_custom_call" | custom-call | flops 226492416 | bytes 2359296 | tf_op jit(solution)/shard_map/chip_part/pallas_call | solution.py:156
  23.1 2.6 %collective-permute-done.refs_1_ = f32[64,512]{1,0:T(8,128)S(1)} collective-permute-done((f32[64,512]{1,0:T(8,128)}, f32[64,512]{1,0:T(8,128)S(1)}, u32[]{:S(2)}, u32[]{:S(2)}) %collective-permute-start) | collective-permute-done | bytes 131104 | tf_op jit(solution)/shard_map/ppermute | solution.py:201
  25.7 0.1 collective-permute-start.3
  25.8 1.2 %collective-permute-done.3.refs_2_ = f32[64,512]{1,0:T(8,128)S(1)} collective-permute-done((f32[64,512]{1,0:T(8,128)S(1)}, f32[64,512]{1,0:T(8,128)S(1)}, u32[]{:S(2)}, u32[]{:S(2)}) %collective-permute-start.3) | collective-permute-done | bytes 131104 | tf_op jit(solution)/shard_map/ppermute | solution.py:206
  27.1 1.0 %far_part.3.own_ref = f32[64,512]{1,0:T(8,128)S(1)} custom-call(bf16[512,2304]{1,0:T(8,128)(2,1)S(1)} %get-tuple-element.16.high_ref, bf16[512,2304]{1,0:T(8,128)(2,1)S(1)} %get-tuple-element.17.low_ref, f32[64,512]{1,0:T(8,128)S(1)} %chip_part.3.part_ref, f32[64,512]{1,0:T(8,128)S(1)} %collective-permute-done.1.refs_0_, ...), custom_call_target="tpu_custom_call" | custom-call | flops 226492416 | bytes 2359296 | tf_op jit(solution)/shard_map/far_part/pallas_call | solution.py:156
  28.1 0.2 collective-permute-start.6
  28.3 7.3 %collective-permute-start.5 = (f32[64,512]{1,0:T(8,128)S(1)}, f32[64,512]{1,0:T(8,128)S(1)}, u32[]{:S(2)}, u32[]{:S(2)}) collective-permute-start(f32[64,512]{1,0:T(8,128)S(1)} %far_part.3.own_ref), channel_id=1, source_target_pairs={{0,3},{1,254},{2,5},{3,0},{4,7},{5,2},{6,9},{7,4},{8,11},{9,6},{10... | collective-permute-start | bytes 393224 | tf_op jit(solution)/shard_map/ppermute | solution.py:202
  35.6 0.0 collective-permute-start.4
  35.6 0.0 collective-permute-done.6.pair_ref
  35.6 0.8 %chip_part.4.part_ref = f32[64,512]{1,0:T(8,128)S(1)} custom-call(bf16[512,2304]{1,0:T(8,128)(2,1)S(1)} %get-tuple-element.16.high_ref, bf16[512,2304]{1,0:T(8,128)(2,1)S(1)} %get-tuple-element.17.low_ref, f32[64,512]{1,0:T(8,128)S(1)} %copy-done, f32[64,512]{1,0:T(8,128)S(1)} %far_part.3.own_ref, f32[64,512]{1,0:T(8,128)S(1)} %collective-permute-done.6.pair_ref), custom_call_target="tpu_custom_call" | custom-call | flops 226492416 | bytes 2359296 | tf_op jit(solution)/shard_map/chip_part/pallas_call | solution.py:156
  36.4 7.6 %collective-permute-done.5 = f32[64,512]{1,0:T(8,128)S(1)} collective-permute-done((f32[64,512]{1,0:T(8,128)S(1)}, f32[64,512]{1,0:T(8,128)S(1)}, u32[]{:S(2)}, u32[]{:S(2)}) %collective-permute-start.5) | collective-permute-done | bytes 131104 | tf_op jit(solution)/shard_map/ppermute | solution.py:202
  44.0 0.0 collective-permute-done.4.refs_0_
  44.0 0.5 collective-permute-start.7
  44.5 1.2 %collective-permute-done.7.refs_1_ = f32[128,512]{1,0:T(8,128)S(1)} collective-permute-done((f32[128,512]{1,0:T(8,128)S(1)}, f32[128,512]{1,0:T(8,128)S(1)}, u32[]{:S(2)}, u32[]{:S(2)}) %collective-permute-start.7) | collective-permute-done | bytes 262176 | tf_op jit(solution)/shard_map/ppermute | solution.py:210
  45.6 1.0 %far_part.4.own_ref = f32[64,512]{1,0:T(8,128)S(1)} custom-call(bf16[512,2304]{1,0:T(8,128)(2,1)S(1)} %get-tuple-element.16.high_ref, bf16[512,2304]{1,0:T(8,128)(2,1)S(1)} %get-tuple-element.17.low_ref, f32[64,512]{1,0:T(8,128)S(1)} %chip_part.4.part_ref, f32[64,512]{1,0:T(8,128)S(1)} %collective-permute-done.4.refs_0_, ...), custom_call_target="tpu_custom_call" | custom-call | flops 226492416 | bytes 2359296 | tf_op jit(solution)/shard_map/far_part/pallas_call | solution.py:156
  46.6 0.5 collective-permute-start.10
  47.1 5.5 %collective-permute-start.9 = (f32[64,512]{1,0:T(8,128)S(1)}, f32[64,512]{1,0:T(8,128)S(1)}, u32[]{:S(2)}, u32[]{:S(2)}) collective-permute-start(f32[64,512]{1,0:T(8,128)S(1)} %far_part.4.own_ref), channel_id=1, source_target_pairs={{0,3},{1,254},{2,5},{3,0},{4,7},{5,2},{6,9},{7,4},{8,11},{9,6},{10... | collective-permute-start | bytes 393224 | tf_op jit(solution)/shard_map/ppermute | solution.py:202
  52.6 0.0 collective-permute-start.8
  52.6 0.0 collective-permute-done.10.pair_ref
  52.6 0.8 %chip_part.5.part_ref = f32[64,512]{1,0:T(8,128)S(1)} custom-call(bf16[512,2304]{1,0:T(8,128)(2,1)S(1)} %get-tuple-element.16.high_ref, bf16[512,2304]{1,0:T(8,128)(2,1)S(1)} %get-tuple-element.17.low_ref, f32[64,512]{1,0:T(8,128)S(1)} %copy-done, f32[64,512]{1,0:T(8,128)S(1)} %far_part.4.own_ref, f32[64,512]{1,0:T(8,128)S(1)} %collective-permute-done.10.pair_ref), custom_call_target="tpu_custom_call" | custom-call | flops 226492416 | bytes 2359296 | tf_op jit(solution)/shard_map/chip_part/pallas_call | solution.py:156
  53.4 6.9 %collective-permute-done.9 = f32[64,512]{1,0:T(8,128)S(1)} collective-permute-done((f32[64,512]{1,0:T(8,128)S(1)}, f32[64,512]{1,0:T(8,128)S(1)}, u32[]{:S(2)}, u32[]{:S(2)}) %collective-permute-start.9) | collective-permute-done | bytes 131104 | tf_op jit(solution)/shard_map/ppermute | solution.py:202
  60.3 0.0 collective-permute-done.8.refs_0_
  60.3 0.5 collective-permute-start.11
  60.8 1.2 %collective-permute-done.11.refs_1_ = f32[128,512]{1,0:T(8,128)S(1)} collective-permute-done((f32[128,512]{1,0:T(8,128)S(1)}, f32[128,512]{1,0:T(8,128)S(1)}, u32[]{:S(2)}, u32[]{:S(2)}) %collective-permute-start.11) | collective-permute-done | bytes 262176 | tf_op jit(solution)/shard_map/ppermute | solution.py:210
  61.9 1.6 %far_part.5 = f32[64,512]{1,0:T(8,128)} custom-call(bf16[512,2304]{1,0:T(8,128)(2,1)S(1)} %get-tuple-element.16.high_ref, bf16[512,2304]{1,0:T(8,128)(2,1)S(1)} %get-tuple-element.17.low_ref, f32[64,512]{1,0:T(8,128)S(1)} %chip_part.5.part_ref, f32[64,512]{1,0:T(8,128)S(1)} %collective-permute-done.8.refs_0_, f32[128,512]{1,0:T(8,128)S(1)} %collective-permute-done.11.refs_1_), custom_call_target="tpu_custom_call" | custom-call | flops 226492416 | bytes 2359296 | tf_op jit(solution)/shard_map/far_part/pallas_call | solution.py:156
  (6 shorter events, 0.0 us)
Async XLA Ops:
  1.5 17.2 %all-to-all-start = ((f32[8,8,512]{2,0,1:T(8,128)}), f32[8,8,512]{2,0,1:T(8,128)S(1)}, u32[]{:S(2)}, u32[]{:S(2)}) async-start(f32[8,8,512]{2,0,1:T(8,128)} %bitcast.5), calls=%async_computation | async-start | bytes 262144 | tf_op jit(solution)/shard_map/all_to_all | solution.py:196
  9.8 12.5 %collective-permute-start.2 = (f32[64,512]{1,0:T(8,128)}, f32[64,512]{1,0:T(8,128)S(1)}, u32[]{:S(2)}, u32[]{:S(2)}) collective-permute-start(f32[64,512]{1,0:T(8,128)} %seeds_ref.5), channel_id=1, source_target_pairs={{0,1},{1,0},{2,3},{3,2},{4,5},{5,4},{6,7},{7,6},{8,9},{9,8},{10,11... | collective-permute-start | bytes 393224 | tf_op jit(solution)/shard_map/ppermute | solution.py:200
  9.8 13.3 %collective-permute-start.1 = (f32[64,512]{1,0:T(8,128)}, f32[64,512]{1,0:T(8,128)S(1)}, u32[]{:S(2)}, u32[]{:S(2)}) collective-permute-start(f32[64,512]{1,0:T(8,128)} %seeds_ref.5), channel_id=1, source_target_pairs={{0,2},{2,4},{3,1},{4,6},{5,3},{6,8},{7,5},{8,10},{9,7},{10,12},{11... | collective-permute-start | bytes 393224 | tf_op jit(solution)/shard_map/ppermute | solution.py:202
  18.7 7.0 %collective-permute-start = (f32[64,512]{1,0:T(8,128)}, f32[64,512]{1,0:T(8,128)S(1)}, u32[]{:S(2)}, u32[]{:S(2)}) collective-permute-start(f32[64,512]{1,0:T(8,128)} %seeds_ref.5), channel_id=1, source_target_pairs={{0,255},{1,2},{2,1},{3,4},{4,3},{5,6},{6,5},{7,8},{8,7},{9,10},{10... | collective-permute-start | bytes 393224 | tf_op jit(solution)/shard_map/ppermute | solution.py:201
  18.7 3.5 %copy-start = (f32[64,512]{1,0:T(8,128)S(1)}, f32[64,512]{1,0:T(8,128)}, u32[]{:S(2)}) copy-start(f32[64,512]{1,0:T(8,128)} %seeds_ref.5) | copy-start | bytes 393220
  25.7 1.3 %collective-permute-start.3 = (f32[64,512]{1,0:T(8,128)S(1)}, f32[64,512]{1,0:T(8,128)S(1)}, u32[]{:S(2)}, u32[]{:S(2)}) collective-permute-start(f32[64,512]{1,0:T(8,128)S(1)} %collective-permute-done.refs_1_), channel_id=1, source_target_pairs={{0,1},{1,0},{2,3},{3,2},{4,5},{5,4},{6,7},{7,6},{8,9},{9,8},{10,11... | collective-permute-start | bytes 393224 | tf_op jit(solution)/shard_map/ppermute | solution.py:206
  28.1 7.5 %collective-permute-start.6 = (f32[64,512]{1,0:T(8,128)S(1)}, f32[64,512]{1,0:T(8,128)S(1)}, u32[]{:S(2)}, u32[]{:S(2)}) collective-permute-start(f32[64,512]{1,0:T(8,128)S(1)} %far_part.3.own_ref), channel_id=1, source_target_pairs={{0,1},{1,0},{2,3},{3,2},{4,5},{5,4},{6,7},{7,6},{8,9},{9,8},{10,11... | collective-permute-start | bytes 393224 | tf_op jit(solution)/shard_map/ppermute | solution.py:200
  28.3 15.7 %collective-permute-start.5 = (f32[64,512]{1,0:T(8,128)S(1)}, f32[64,512]{1,0:T(8,128)S(1)}, u32[]{:S(2)}, u32[]{:S(2)}) collective-permute-start(f32[64,512]{1,0:T(8,128)S(1)} %far_part.3.own_ref), channel_id=1, source_target_pairs={{0,3},{1,254},{2,5},{3,0},{4,7},{5,2},{6,9},{7,4},{8,11},{9,6},{10... | collective-permute-start | bytes 393224 | tf_op jit(solution)/shard_map/ppermute | solution.py:202
  35.6 8.4 %collective-permute-start.4 = (f32[64,512]{1,0:T(8,128)S(1)}, f32[64,512]{1,0:T(8,128)S(1)}, u32[]{:S(2)}, u32[]{:S(2)}) collective-permute-start(f32[64,512]{1,0:T(8,128)S(1)} %far_part.3.own_ref), channel_id=1, source_target_pairs={{0,255},{1,2},{2,1},{3,4},{4,3},{5,6},{6,5},{7,8},{8,7},{9,10},{10... | collective-permute-start | bytes 393224 | tf_op jit(solution)/shard_map/ppermute | solution.py:201
  44.0 1.6 %collective-permute-start.7 = (f32[128,512]{1,0:T(8,128)S(1)}, f32[128,512]{1,0:T(8,128)S(1)}, u32[]{:S(2)}, u32[]{:S(2)}) collective-permute-start(f32[128,512]{1,0:T(8,128)S(1)} %pad_maximum_fusion), channel_id=1, source_target_pairs={{0,1},{1,0},{2,3},{3,2},{4,5},{5,4},{6,7},{7,6},{8,9},{9,8},{10,11... | collective-permute-start | bytes 786440 | tf_op jit(solution)/shard_map/ppermute | solution.py:210
  46.6 6.0 %collective-permute-start.10 = (f32[64,512]{1,0:T(8,128)S(1)}, f32[64,512]{1,0:T(8,128)S(1)}, u32[]{:S(2)}, u32[]{:S(2)}) collective-permute-start(f32[64,512]{1,0:T(8,128)S(1)} %far_part.4.own_ref), channel_id=1, source_target_pairs={{0,1},{1,0},{2,3},{3,2},{4,5},{5,4},{6,7},{7,6},{8,9},{9,8},{10,11... | collective-permute-start | bytes 393224 | tf_op jit(solution)/shard_map/ppermute | solution.py:200
  47.1 13.2 %collective-permute-start.9 = (f32[64,512]{1,0:T(8,128)S(1)}, f32[64,512]{1,0:T(8,128)S(1)}, u32[]{:S(2)}, u32[]{:S(2)}) collective-permute-start(f32[64,512]{1,0:T(8,128)S(1)} %far_part.4.own_ref), channel_id=1, source_target_pairs={{0,3},{1,254},{2,5},{3,0},{4,7},{5,2},{6,9},{7,4},{8,11},{9,6},{10... | collective-permute-start | bytes 393224 | tf_op jit(solution)/shard_map/ppermute | solution.py:202
  52.6 7.7 %collective-permute-start.8 = (f32[64,512]{1,0:T(8,128)S(1)}, f32[64,512]{1,0:T(8,128)S(1)}, u32[]{:S(2)}, u32[]{:S(2)}) collective-permute-start(f32[64,512]{1,0:T(8,128)S(1)} %far_part.4.own_ref), channel_id=1, source_target_pairs={{0,255},{1,2},{2,1},{3,4},{4,3},{5,6},{6,5},{7,8},{8,7},{9,10},{10... | collective-permute-start | bytes 393224 | tf_op jit(solution)/shard_map/ppermute | solution.py:201
  60.3 1.6 %collective-permute-start.11 = (f32[128,512]{1,0:T(8,128)S(1)}, f32[128,512]{1,0:T(8,128)S(1)}, u32[]{:S(2)}, u32[]{:S(2)}) collective-permute-start(f32[128,512]{1,0:T(8,128)S(1)} %pad_maximum_fusion.1), channel_id=1, source_target_pairs={{0,1},{1,0},{2,3},{3,2},{4,5},{5,4},{6,7},{7,6},{8,9},{9,8},{10,11... | collective-permute-start | bytes 786440 | tf_op jit(solution)/shard_map/ppermute | solution.py:210

commit v6 on v5

--- a/solution.py
+++ b/solution.py
@@ -74,7 +74,7 @@
             low_ref[pl.ds(at, 16), columns] = (both - high.astype(jnp.float32)).astype(jnp.bfloat16)
         return 0
 
-    lax.fori_loop(0, events // 16, sixteen, 0, unroll=8)
+    lax.fori_loop(0, events // 16, sixteen, 0, unroll=16)
 
 
 def build(edges):

time: 63.8 us -> 63.8 us (level)
  no operation moved by 1% of the time
where the time goes in v6:
time: 63.8 us; the launch traced here: 63.6 us
  starting transfers between devices  31.8 us (50%)
  waiting for transfers between devices  21 us (33%)
  Pallas kernels  10.7 us (17%)
    ppermute x3, starting transfers between devices, on_device(): away = lax.ppermute(scores, AXES, skip if step == 0 else ring(3))  21.7 us
    ppermute x3, waiting for transfers between devices, on_device(): away = lax.ppermute(scores, AXES, skip if step == 0 else ring(3))  14.5 us
    all_to_all x1, starting transfers between devices, on_device(): lax.all_to_all(edges, 'cols', split_axis=1, concat_axis=0, tiled=True)  8.24 us
    pallas_call x6, Pallas kernels, call(): pl.pallas_call(kernel, out_shape=jax.ShapeDtypeStruct(seeds.shape, jnp.fl...  6.02 us
    pallas_call x1, Pallas kernels, build(): pl.pallas_call(build_kernel, out_shape=(out, out), scratch_shapes=[pltpu....  3.12 us
    ppermute x3, waiting for transfers between devices, on_device(): near = lax.ppermute(scores, AXES, ring(-1))  3.01 us
    ppermute x2, waiting for transfers between devices, on_device(): cross = lax.ppermute(jnp.concatenate([near, away], axis=0), AXES, on_chip)  2.32 us
    pallas_call x1, Pallas kernels, pack(): pl.pallas_call(pack_kernel, out_shape=jax.ShapeDtypeStruct((2 * slots, ev...  1.54 us
  transfers between devices with their start and end apart: 13, of which 6 were waited for; matrix products, arithmetic and copies ran while one was open for 0% of the time, Pallas kernels for 9%

profile of v6, /device:TPU:33, one launch (start us, length us, event | category | flops | bytes accessed | tf_op | source)
XLA Modules:
  0.0 63.6 jit_solution(3108969418243975353)
XLA Ops:
  0.0 1.5 %pack.1 = f32[8,4096]{1,0:T(8,128)} custom-call(s32[4,4096]{1,0:T(4,128)} %offsets_ref.1, f32[4,4096]{1,0:T(4,128)} %weights_ref.1), custom_call_target="tpu_custom_call" | custom-call | tf_op jit(solution)/shard_map/pack/pallas_call | solution.py:183
  1.5 8.2 %all-to-all-start = ((f32[8,8,512]{2,0,1:T(8,128)}), f32[8,8,512]{2,0,1:T(8,128)S(1)}, u32[]{:S(2)}, u32[]{:S(2)}) async-start(f32[8,8,512]{2,0,1:T(8,128)} %bitcast.5), calls=%async_computation | async-start | bytes 262144 | tf_op jit(solution)/shard_map/all_to_all | solution.py:196
  9.8 0.0 collective-permute-start.2
  9.8 8.9 %collective-permute-start.1 = (f32[64,512]{1,0:T(8,128)}, f32[64,512]{1,0:T(8,128)S(1)}, u32[]{:S(2)}, u32[]{:S(2)}) collective-permute-start(f32[64,512]{1,0:T(8,128)} %seeds_ref.5), channel_id=1, source_target_pairs={{0,2},{2,4},{3,1},{4,6},{5,3},{6,8},{7,5},{8,10},{9,7},{10,12},{11... | collective-permute-start | bytes 393224 | tf_op jit(solution)/shard_map/ppermute | solution.py:202
  18.7 0.0 collective-permute-start
  18.7 0.0 all-to-all-done
  18.7 3.1 %build.1 = (bf16[512,2304]{1,0:T(8,128)(2,1)S(1)}, bf16[512,2304]{1,0:T(8,128)(2,1)S(1)}) custom-call(f32[64,512]{1,0:T(8,128)S(1)} %bitcast.4), custom_call_target="tpu_custom_call" | custom-call | flops 3000000000 | bytes 4718592 | tf_op jit(solution)/shard_map/build/pallas_call | solution.py:83
  21.9 0.0 collective-permute-done.2.pair_ref
  21.9 0.8 %chip_part.3.part_ref = f32[64,512]{1,0:T(8,128)S(1)} custom-call(bf16[512,2304]{1,0:T(8,128)(2,1)S(1)} %get-tuple-element.16.high_ref, bf16[512,2304]{1,0:T(8,128)(2,1)S(1)} %get-tuple-element.17.low_ref, f32[64,512]{1,0:T(8,128)S(1)} %copy-done, f32[64,512]{1,0:T(8,128)S(1)} %copy-done, f32[64,512]{1,0:T(8,128)S(1)} %collective-permute-done.2.pair_ref), custom_call_target="tpu_custom_call" | custom-call | flops 226492416 | bytes 2359296 | tf_op jit(solution)/shard_map/chip_part/pallas_call | solution.py:156
  22.7 3.0 %collective-permute-done.refs_1_ = f32[64,512]{1,0:T(8,128)S(1)} collective-permute-done((f32[64,512]{1,0:T(8,128)}, f32[64,512]{1,0:T(8,128)S(1)}, u32[]{:S(2)}, u32[]{:S(2)}) %collective-permute-start) | collective-permute-done | bytes 131104 | tf_op jit(solution)/shard_map/ppermute | solution.py:201
  25.7 0.1 collective-permute-start.3
  25.8 1.2 %collective-permute-done.3.refs_2_ = f32[64,512]{1,0:T(8,128)S(1)} collective-permute-done((f32[64,512]{1,0:T(8,128)S(1)}, f32[64,512]{1,0:T(8,128)S(1)}, u32[]{:S(2)}, u32[]{:S(2)}) %collective-permute-start.3) | collective-permute-done | bytes 131104 | tf_op jit(solution)/shard_map/ppermute | solution.py:206
  27.1 1.0 %far_part.3.own_ref = f32[64,512]{1,0:T(8,128)S(1)} custom-call(bf16[512,2304]{1,0:T(8,128)(2,1)S(1)} %get-tuple-element.16.high_ref, bf16[512,2304]{1,0:T(8,128)(2,1)S(1)} %get-tuple-element.17.low_ref, f32[64,512]{1,0:T(8,128)S(1)} %chip_part.3.part_ref, f32[64,512]{1,0:T(8,128)S(1)} %collective-permute-done.1.refs_0_, ...), custom_call_target="tpu_custom_call" | custom-call | flops 226492416 | bytes 2359296 | tf_op jit(solution)/shard_map/far_part/pallas_call | solution.py:156
  28.1 0.2 collective-permute-start.6
  28.3 7.3 %collective-permute-start.5 = (f32[64,512]{1,0:T(8,128)S(1)}, f32[64,512]{1,0:T(8,128)S(1)}, u32[]{:S(2)}, u32[]{:S(2)}) collective-permute-start(f32[64,512]{1,0:T(8,128)S(1)} %far_part.3.own_ref), channel_id=1, source_target_pairs={{0,3},{1,254},{2,5},{3,0},{4,7},{5,2},{6,9},{7,4},{8,11},{9,6},{10... | collective-permute-start | bytes 393224 | tf_op jit(solution)/shard_map/ppermute | solution.py:202
  35.6 0.0 collective-permute-start.4
  35.6 0.0 collective-permute-done.6.pair_ref
  35.6 0.8 %chip_part.4.part_ref = f32[64,512]{1,0:T(8,128)S(1)} custom-call(bf16[512,2304]{1,0:T(8,128)(2,1)S(1)} %get-tuple-element.16.high_ref, bf16[512,2304]{1,0:T(8,128)(2,1)S(1)} %get-tuple-element.17.low_ref, f32[64,512]{1,0:T(8,128)S(1)} %copy-done, f32[64,512]{1,0:T(8,128)S(1)} %far_part.3.own_ref, f32[64,512]{1,0:T(8,128)S(1)} %collective-permute-done.6.pair_ref), custom_call_target="tpu_custom_call" | custom-call | flops 226492416 | bytes 2359296 | tf_op jit(solution)/shard_map/chip_part/pallas_call | solution.py:156
  36.4 7.6 %collective-permute-done.5 = f32[64,512]{1,0:T(8,128)S(1)} collective-permute-done((f32[64,512]{1,0:T(8,128)S(1)}, f32[64,512]{1,0:T(8,128)S(1)}, u32[]{:S(2)}, u32[]{:S(2)}) %collective-permute-start.5) | collective-permute-done | bytes 131104 | tf_op jit(solution)/shard_map/ppermute | solution.py:202
  44.0 0.5 collective-permute-start.7
  44.5 1.2 %collective-permute-done.7.refs_1_ = f32[128,512]{1,0:T(8,128)S(1)} collective-permute-done((f32[128,512]{1,0:T(8,128)S(1)}, f32[128,512]{1,0:T(8,128)S(1)}, u32[]{:S(2)}, u32[]{:S(2)}) %collective-permute-start.7) | collective-permute-done | bytes 262176 | tf_op jit(solution)/shard_map/ppermute | solution.py:210
  45.6 1.0 %far_part.4.own_ref = f32[64,512]{1,0:T(8,128)S(1)} custom-call(bf16[512,2304]{1,0:T(8,128)(2,1)S(1)} %get-tuple-element.16.high_ref, bf16[512,2304]{1,0:T(8,128)(2,1)S(1)} %get-tuple-element.17.low_ref, f32[64,512]{1,0:T(8,128)S(1)} %chip_part.4.part_ref, f32[64,512]{1,0:T(8,128)S(1)} %collective-permute-done.4.refs_0_, ...), custom_call_target="tpu_custom_call" | custom-call | flops 226492416 | bytes 2359296 | tf_op jit(solution)/shard_map/far_part/pallas_call | solution.py:156
  46.6 0.5 collective-permute-start.10
  47.1 5.5 %collective-permute-start.9 = (f32[64,512]{1,0:T(8,128)S(1)}, f32[64,512]{1,0:T(8,128)S(1)}, u32[]{:S(2)}, u32[]{:S(2)}) collective-permute-start(f32[64,512]{1,0:T(8,128)S(1)} %far_part.4.own_ref), channel_id=1, source_target_pairs={{0,3},{1,254},{2,5},{3,0},{4,7},{5,2},{6,9},{7,4},{8,11},{9,6},{10... | collective-permute-start | bytes 393224 | tf_op jit(solution)/shard_map/ppermute | solution.py:202
  52.6 0.0 collective-permute-start.8
  52.6 0.0 collective-permute-done.10.pair_ref
  52.6 0.8 %chip_part.5.part_ref = f32[64,512]{1,0:T(8,128)S(1)} custom-call(bf16[512,2304]{1,0:T(8,128)(2,1)S(1)} %get-tuple-element.16.high_ref, bf16[512,2304]{1,0:T(8,128)(2,1)S(1)} %get-tuple-element.17.low_ref, f32[64,512]{1,0:T(8,128)S(1)} %copy-done, f32[64,512]{1,0:T(8,128)S(1)} %far_part.4.own_ref, f32[64,512]{1,0:T(8,128)S(1)} %collective-permute-done.10.pair_ref), custom_call_target="tpu_custom_call" | custom-call | flops 226492416 | bytes 2359296 | tf_op jit(solution)/shard_map/chip_part/pallas_call | solution.py:156
  53.4 6.9 %collective-permute-done.9 = f32[64,512]{1,0:T(8,128)S(1)} collective-permute-done((f32[64,512]{1,0:T(8,128)S(1)}, f32[64,512]{1,0:T(8,128)S(1)}, u32[]{:S(2)}, u32[]{:S(2)}) %collective-permute-start.9) | collective-permute-done | bytes 131104 | tf_op jit(solution)/shard_map/ppermute | solution.py:202
  60.3 0.0 collective-permute-done.8.refs_0_
  60.3 0.5 collective-permute-start.11
  60.8 1.2 %collective-permute-done.11.refs_1_ = f32[128,512]{1,0:T(8,128)S(1)} collective-permute-done((f32[128,512]{1,0:T(8,128)S(1)}, f32[128,512]{1,0:T(8,128)S(1)}, u32[]{:S(2)}, u32[]{:S(2)}) %collective-permute-start.11) | collective-permute-done | bytes 262176 | tf_op jit(solution)/shard_map/ppermute | solution.py:210
  61.9 1.6 %far_part.5 = f32[64,512]{1,0:T(8,128)} custom-call(bf16[512,2304]{1,0:T(8,128)(2,1)S(1)} %get-tuple-element.16.high_ref, bf16[512,2304]{1,0:T(8,128)(2,1)S(1)} %get-tuple-element.17.low_ref, f32[64,512]{1,0:T(8,128)S(1)} %chip_part.5.part_ref, f32[64,512]{1,0:T(8,128)S(1)} %collective-permute-done.8.refs_0_, f32[128,512]{1,0:T(8,128)S(1)} %collective-permute-done.11.refs_1_), custom_call_target="tpu_custom_call" | custom-call | flops 226492416 | bytes 2359296 | tf_op jit(solution)/shard_map/far_part/pallas_call | solution.py:156
  (6 shorter events, 0.0 us)
Async XLA Ops:
  1.5 17.2 %all-to-all-start = ((f32[8,8,512]{2,0,1:T(8,128)}), f32[8,8,512]{2,0,1:T(8,128)S(1)}, u32[]{:S(2)}, u32[]{:S(2)}) async-start(f32[8,8,512]{2,0,1:T(8,128)} %bitcast.5), calls=%async_computation | async-start | bytes 262144 | tf_op jit(solution)/shard_map/all_to_all | solution.py:196
  9.8 12.1 %collective-permute-start.2 = (f32[64,512]{1,0:T(8,128)}, f32[64,512]{1,0:T(8,128)S(1)}, u32[]{:S(2)}, u32[]{:S(2)}) collective-permute-start(f32[64,512]{1,0:T(8,128)} %seeds_ref.5), channel_id=1, source_target_pairs={{0,1},{1,0},{2,3},{3,2},{4,5},{5,4},{6,7},{7,6},{8,9},{9,8},{10,11... | collective-permute-start | bytes 393224 | tf_op jit(solution)/shard_map/ppermute | solution.py:200
  9.8 12.9 %collective-permute-start.1 = (f32[64,512]{1,0:T(8,128)}, f32[64,512]{1,0:T(8,128)S(1)}, u32[]{:S(2)}, u32[]{:S(2)}) collective-permute-start(f32[64,512]{1,0:T(8,128)} %seeds_ref.5), channel_id=1, source_target_pairs={{0,2},{2,4},{3,1},{4,6},{5,3},{6,8},{7,5},{8,10},{9,7},{10,12},{11... | collective-permute-start | bytes 393224 | tf_op jit(solution)/shard_map/ppermute | solution.py:202
  18.7 7.0 %collective-permute-start = (f32[64,512]{1,0:T(8,128)}, f32[64,512]{1,0:T(8,128)S(1)}, u32[]{:S(2)}, u32[]{:S(2)}) collective-permute-start(f32[64,512]{1,0:T(8,128)} %seeds_ref.5), channel_id=1, source_target_pairs={{0,255},{1,2},{2,1},{3,4},{4,3},{5,6},{6,5},{7,8},{8,7},{9,10},{10... | collective-permute-start | bytes 393224 | tf_op jit(solution)/shard_map/ppermute | solution.py:201
  18.7 3.1 %copy-start = (f32[64,512]{1,0:T(8,128)S(1)}, f32[64,512]{1,0:T(8,128)}, u32[]{:S(2)}) copy-start(f32[64,512]{1,0:T(8,128)} %seeds_ref.5) | copy-start | bytes 393220
  25.7 1.3 %collective-permute-start.3 = (f32[64,512]{1,0:T(8,128)S(1)}, f32[64,512]{1,0:T(8,128)S(1)}, u32[]{:S(2)}, u32[]{:S(2)}) collective-permute-start(f32[64,512]{1,0:T(8,128)S(1)} %collective-permute-done.refs_1_), channel_id=1, source_target_pairs={{0,1},{1,0},{2,3},{3,2},{4,5},{5,4},{6,7},{7,6},{8,9},{9,8},{10,11... | collective-permute-start | bytes 393224 | tf_op jit(solution)/shard_map/ppermute | solution.py:206
  28.1 7.5 %collective-permute-start.6 = (f32[64,512]{1,0:T(8,128)S(1)}, f32[64,512]{1,0:T(8,128)S(1)}, u32[]{:S(2)}, u32[]{:S(2)}) collective-permute-start(f32[64,512]{1,0:T(8,128)S(1)} %far_part.3.own_ref), channel_id=1, source_target_pairs={{0,1},{1,0},{2,3},{3,2},{4,5},{5,4},{6,7},{7,6},{8,9},{9,8},{10,11... | collective-permute-start | bytes 393224 | tf_op jit(solution)/shard_map/ppermute | solution.py:200
  28.3 15.7 %collective-permute-start.5 = (f32[64,512]{1,0:T(8,128)S(1)}, f32[64,512]{1,0:T(8,128)S(1)}, u32[]{:S(2)}, u32[]{:S(2)}) collective-permute-start(f32[64,512]{1,0:T(8,128)S(1)} %far_part.3.own_ref), channel_id=1, source_target_pairs={{0,3},{1,254},{2,5},{3,0},{4,7},{5,2},{6,9},{7,4},{8,11},{9,6},{10... | collective-permute-start | bytes 393224 | tf_op jit(solution)/shard_map/ppermute | solution.py:202
  35.6 8.4 %collective-permute-start.4 = (f32[64,512]{1,0:T(8,128)S(1)}, f32[64,512]{1,0:T(8,128)S(1)}, u32[]{:S(2)}, u32[]{:S(2)}) collective-permute-start(f32[64,512]{1,0:T(8,128)S(1)} %far_part.3.own_ref), channel_id=1, source_target_pairs={{0,255},{1,2},{2,1},{3,4},{4,3},{5,6},{6,5},{7,8},{8,7},{9,10},{10... | collective-permute-start | bytes 393224 | tf_op jit(solution)/shard_map/ppermute | solution.py:201
  44.0 1.6 %collective-permute-start.7 = (f32[128,512]{1,0:T(8,128)S(1)}, f32[128,512]{1,0:T(8,128)S(1)}, u32[]{:S(2)}, u32[]{:S(2)}) collective-permute-start(f32[128,512]{1,0:T(8,128)S(1)} %pad_maximum_fusion), channel_id=1, source_target_pairs={{0,1},{1,0},{2,3},{3,2},{4,5},{5,4},{6,7},{7,6},{8,9},{9,8},{10,11... | collective-permute-start | bytes 786440 | tf_op jit(solution)/shard_map/ppermute | solution.py:210
  46.6 6.0 %collective-permute-start.10 = (f32[64,512]{1,0:T(8,128)S(1)}, f32[64,512]{1,0:T(8,128)S(1)}, u32[]{:S(2)}, u32[]{:S(2)}) collective-permute-start(f32[64,512]{1,0:T(8,128)S(1)} %far_part.4.own_ref), channel_id=1, source_target_pairs={{0,1},{1,0},{2,3},{3,2},{4,5},{5,4},{6,7},{7,6},{8,9},{9,8},{10,11... | collective-permute-start | bytes 393224 | tf_op jit(solution)/shard_map/ppermute | solution.py:200
  47.1 13.2 %collective-permute-start.9 = (f32[64,512]{1,0:T(8,128)S(1)}, f32[64,512]{1,0:T(8,128)S(1)}, u32[]{:S(2)}, u32[]{:S(2)}) collective-permute-start(f32[64,512]{1,0:T(8,128)S(1)} %far_part.4.own_ref), channel_id=1, source_target_pairs={{0,3},{1,254},{2,5},{3,0},{4,7},{5,2},{6,9},{7,4},{8,11},{9,6},{10... | collective-permute-start | bytes 393224 | tf_op jit(solution)/shard_map/ppermute | solution.py:202
  52.6 7.7 %collective-permute-start.8 = (f32[64,512]{1,0:T(8,128)S(1)}, f32[64,512]{1,0:T(8,128)S(1)}, u32[]{:S(2)}, u32[]{:S(2)}) collective-permute-start(f32[64,512]{1,0:T(8,128)S(1)} %far_part.4.own_ref), channel_id=1, source_target_pairs={{0,255},{1,2},{2,1},{3,4},{4,3},{5,6},{6,5},{7,8},{8,7},{9,10},{10... | collective-permute-start | bytes 393224 | tf_op jit(solution)/shard_map/ppermute | solution.py:201
  60.3 1.6 %collective-permute-start.11 = (f32[128,512]{1,0:T(8,128)S(1)}, f32[128,512]{1,0:T(8,128)S(1)}, u32[]{:S(2)}, u32[]{:S(2)}) collective-permute-start(f32[128,512]{1,0:T(8,128)S(1)} %pad_maximum_fusion.1), channel_id=1, source_target_pairs={{0,1},{1,0},{2,3},{3,2},{4,5},{5,4},{6,7},{7,6},{8,9},{9,8},{10,11... | collective-permute-start | bytes 786440 | tf_op jit(solution)/shard_map/ppermute | solution.py:210

commit v7 on v6

--- a/solution.py
+++ b/solution.py
@@ -207,8 +207,8 @@
             scores = far_part(matrix, seeds, part, [away, near, cross], (0, 1, 4), count)
         else:
             near, away, part = lax.optimization_barrier((near, away, part))
-            cross = lax.ppermute(jnp.concatenate([near, away], axis=0), AXES, on_chip)
-            scores = far_part(matrix, seeds, part, [near, cross], (1, 4, 0), count)
+            cross = [lax.ppermute(block, AXES, on_chip) for block in (near, away)]
+            scores = far_part(matrix, seeds, part, [near, *cross], (1, 4, 0), count)
     return scores
 
 

time: 63.8 us -> 63.9 us (level)
    ppermute x2 -> x4, waiting for transfers between devices: 2.32 us -> 2.46 us  [on_device(): cross = [lax.ppermute(block, AXES, on_chip) for block in (near, away)]]
  transfers between devices with their start and end apart: 13 -> 15, of which waited for: 6 -> 8; matrix products, arithmetic and copies ran while one was open for 0% -> 0% of each run, Pallas kernels for 9% -> 9%
where the time goes in v7:
time: 63.9 us; the launch traced here: 63.6 us
  starting transfers between devices  31.8 us (50%)
  waiting for transfers between devices  21.1 us (33%)
  Pallas kernels  10.7 us (17%)
    ppermute x3, starting transfers between devices, on_device(): away = lax.ppermute(scores, AXES, skip if step == 0 else ring(3))  21.9 us
    ppermute x3, waiting for transfers between devices, on_device(): away = lax.ppermute(scores, AXES, skip if step == 0 else ring(3))  14.4 us
    all_to_all x1, starting transfers between devices, on_device(): lax.all_to_all(edges, 'cols', split_axis=1, concat_axis=0, tiled=True)  8.24 us
    pallas_call x6, Pallas kernels, call(): pl.pallas_call(kernel, out_shape=jax.ShapeDtypeStruct(seeds.shape, jnp.fl...  6.02 us
    pallas_call x1, Pallas kernels, build(): pl.pallas_call(build_kernel, out_shape=(out, out), scratch_shapes=[pltpu....  3.12 us
    ppermute x3, waiting for transfers between devices, on_device(): near = lax.ppermute(scores, AXES, ring(-1))  3.01 us
    ppermute x4, waiting for transfers between devices, on_device(): cross = [lax.ppermute(block, AXES, on_chip) for block in (near, away)]  2.46 us
    pallas_call x1, Pallas kernels, pack(): pl.pallas_call(pack_kernel, out_shape=jax.ShapeDtypeStruct((2 * slots, ev...  1.54 us
  transfers between devices with their start and end apart: 15, of which 8 were waited for; matrix products, arithmetic and copies ran while one was open for 0% of the time, Pallas kernels for 9%

profile of v7, /device:TPU:33, one launch (start us, length us, event | category | flops | bytes accessed | tf_op | source)
XLA Modules:
  0.0 63.6 jit_solution(13019364409381791515)
XLA Ops:
  0.0 1.5 %pack.1 = f32[8,4096]{1,0:T(8,128)} custom-call(s32[4,4096]{1,0:T(4,128)} %offsets_ref.1, f32[4,4096]{1,0:T(4,128)} %weights_ref.1), custom_call_target="tpu_custom_call" | custom-call | tf_op jit(solution)/shard_map/pack/pallas_call | solution.py:183
  1.5 8.2 %all-to-all-start = ((f32[8,8,512]{2,0,1:T(8,128)}), f32[8,8,512]{2,0,1:T(8,128)S(1)}, u32[]{:S(2)}, u32[]{:S(2)}) async-start(f32[8,8,512]{2,0,1:T(8,128)} %bitcast.5), calls=%async_computation | async-start | bytes 262144 | tf_op jit(solution)/shard_map/all_to_all | solution.py:196
  9.8 0.0 collective-permute-start.2
  9.8 8.9 %collective-permute-start.1 = (f32[64,512]{1,0:T(8,128)}, f32[64,512]{1,0:T(8,128)S(1)}, u32[]{:S(2)}, u32[]{:S(2)}) collective-permute-start(f32[64,512]{1,0:T(8,128)} %seeds_ref.5), channel_id=1, source_target_pairs={{0,2},{2,4},{3,1},{4,6},{5,3},{6,8},{7,5},{8,10},{9,7},{10,12},{11... | collective-permute-start | bytes 393224 | tf_op jit(solution)/shard_map/ppermute | solution.py:202
  18.7 0.0 collective-permute-start
  18.7 0.0 all-to-all-done
  18.7 3.1 %build.1 = (bf16[512,2304]{1,0:T(8,128)(2,1)S(1)}, bf16[512,2304]{1,0:T(8,128)(2,1)S(1)}) custom-call(f32[64,512]{1,0:T(8,128)S(1)} %bitcast.4), custom_call_target="tpu_custom_call" | custom-call | flops 3000000000 | bytes 4718592 | tf_op jit(solution)/shard_map/build/pallas_call | solution.py:83
  21.9 0.0 collective-permute-done.2.pair_ref
  21.9 0.8 %chip_part.3.part_ref = f32[64,512]{1,0:T(8,128)S(1)} custom-call(bf16[512,2304]{1,0:T(8,128)(2,1)S(1)} %get-tuple-element.16.high_ref, bf16[512,2304]{1,0:T(8,128)(2,1)S(1)} %get-tuple-element.17.low_ref, f32[64,512]{1,0:T(8,128)S(1)} %copy-done, f32[64,512]{1,0:T(8,128)S(1)} %copy-done, f32[64,512]{1,0:T(8,128)S(1)} %collective-permute-done.2.pair_ref), custom_call_target="tpu_custom_call" | custom-call | flops 226492416 | bytes 2359296 | tf_op jit(solution)/shard_map/chip_part/pallas_call | solution.py:156
  22.7 3.0 %collective-permute-done.refs_1_ = f32[64,512]{1,0:T(8,128)S(1)} collective-permute-done((f32[64,512]{1,0:T(8,128)}, f32[64,512]{1,0:T(8,128)S(1)}, u32[]{:S(2)}, u32[]{:S(2)}) %collective-permute-start) | collective-permute-done | bytes 131104 | tf_op jit(solution)/shard_map/ppermute | solution.py:201
  25.7 0.1 collective-permute-start.3
  25.8 1.2 %collective-permute-done.3.refs_2_ = f32[64,512]{1,0:T(8,128)S(1)} collective-permute-done((f32[64,512]{1,0:T(8,128)S(1)}, f32[64,512]{1,0:T(8,128)S(1)}, u32[]{:S(2)}, u32[]{:S(2)}) %collective-permute-start.3) | collective-permute-done | bytes 131104 | tf_op jit(solution)/shard_map/ppermute | solution.py:206
  27.1 1.0 %far_part.3.own_ref = f32[64,512]{1,0:T(8,128)S(1)} custom-call(bf16[512,2304]{1,0:T(8,128)(2,1)S(1)} %get-tuple-element.16.high_ref, bf16[512,2304]{1,0:T(8,128)(2,1)S(1)} %get-tuple-element.17.low_ref, f32[64,512]{1,0:T(8,128)S(1)} %chip_part.3.part_ref, f32[64,512]{1,0:T(8,128)S(1)} %collective-permute-done.1.refs_0_, ...), custom_call_target="tpu_custom_call" | custom-call | flops 226492416 | bytes 2359296 | tf_op jit(solution)/shard_map/far_part/pallas_call | solution.py:156
  28.1 0.2 collective-permute-start.6
  28.3 7.3 %collective-permute-start.5 = (f32[64,512]{1,0:T(8,128)S(1)}, f32[64,512]{1,0:T(8,128)S(1)}, u32[]{:S(2)}, u32[]{:S(2)}) collective-permute-start(f32[64,512]{1,0:T(8,128)S(1)} %far_part.3.own_ref), channel_id=1, source_target_pairs={{0,3},{1,254},{2,5},{3,0},{4,7},{5,2},{6,9},{7,4},{8,11},{9,6},{10... | collective-permute-start | bytes 393224 | tf_op jit(solution)/shard_map/ppermute | solution.py:202
  35.6 0.0 collective-permute-start.4
  35.6 0.8 %chip_part.4.part_ref = f32[64,512]{1,0:T(8,128)S(1)} custom-call(bf16[512,2304]{1,0:T(8,128)(2,1)S(1)} %get-tuple-element.16.high_ref, bf16[512,2304]{1,0:T(8,128)(2,1)S(1)} %get-tuple-element.17.low_ref, f32[64,512]{1,0:T(8,128)S(1)} %copy-done, f32[64,512]{1,0:T(8,128)S(1)} %far_part.3.own_ref, f32[64,512]{1,0:T(8,128)S(1)} %collective-permute-done.6.pair_ref), custom_call_target="tpu_custom_call" | custom-call | flops 226492416 | bytes 2359296 | tf_op jit(solution)/shard_map/chip_part/pallas_call | solution.py:156
  36.4 7.6 %collective-permute-done.5 = f32[64,512]{1,0:T(8,128)S(1)} collective-permute-done((f32[64,512]{1,0:T(8,128)S(1)}, f32[64,512]{1,0:T(8,128)S(1)}, u32[]{:S(2)}, u32[]{:S(2)}) %collective-permute-start.5) | collective-permute-done | bytes 131104 | tf_op jit(solution)/shard_map/ppermute | solution.py:202
  44.0 0.4 collective-permute-start.8
  44.4 0.1 collective-permute-start.7
  44.5 0.9 %collective-permute-done.8.refs_2_ = f32[64,512]{1,0:T(8,128)S(1)} collective-permute-done((f32[64,512]{1,0:T(8,128)S(1)}, f32[64,512]{1,0:T(8,128)S(1)}, u32[]{:S(2)}, u32[]{:S(2)}) %collective-permute-start.8) | collective-permute-done | bytes 131104 | tf_op jit(solution)/shard_map/ppermute | solution.py:210
  45.3 0.4 collective-permute-done.7.refs_1_
  45.7 1.0 %far_part.4.own_ref = f32[64,512]{1,0:T(8,128)S(1)} custom-call(bf16[512,2304]{1,0:T(8,128)(2,1)S(1)} %get-tuple-element.16.high_ref, bf16[512,2304]{1,0:T(8,128)(2,1)S(1)} %get-tuple-element.17.low_ref, f32[64,512]{1,0:T(8,128)S(1)} %chip_part.4.part_ref, f32[64,512]{1,0:T(8,128)S(1)} %collective-permute-done.4.refs_0_, ...), custom_call_target="tpu_custom_call" | custom-call | flops 226492416 | bytes 2359296 | tf_op jit(solution)/shard_map/far_part/pallas_call | solution.py:156
  46.7 0.3 collective-permute-start.11
  47.0 5.7 %collective-permute-start.10 = (f32[64,512]{1,0:T(8,128)S(1)}, f32[64,512]{1,0:T(8,128)S(1)}, u32[]{:S(2)}, u32[]{:S(2)}) collective-permute-start(f32[64,512]{1,0:T(8,128)S(1)} %far_part.4.own_ref), channel_id=1, source_target_pairs={{0,3},{1,254},{2,5},{3,0},{4,7},{5,2},{6,9},{7,4},{8,11},{9,6},{10... | collective-permute-start | bytes 393224 | tf_op jit(solution)/shard_map/ppermute | solution.py:202
  52.7 0.8 %chip_part.5.part_ref = f32[64,512]{1,0:T(8,128)S(1)} custom-call(bf16[512,2304]{1,0:T(8,128)(2,1)S(1)} %get-tuple-element.16.high_ref, bf16[512,2304]{1,0:T(8,128)(2,1)S(1)} %get-tuple-element.17.low_ref, f32[64,512]{1,0:T(8,128)S(1)} %copy-done, f32[64,512]{1,0:T(8,128)S(1)} %far_part.4.own_ref, f32[64,512]{1,0:T(8,128)S(1)} %collective-permute-done.11.pair_ref), custom_call_target="tpu_custom_call" | custom-call | flops 226492416 | bytes 2359296 | tf_op jit(solution)/shard_map/chip_part/pallas_call | solution.py:156
  53.4 6.8 %collective-permute-done.10 = f32[64,512]{1,0:T(8,128)S(1)} collective-permute-done((f32[64,512]{1,0:T(8,128)S(1)}, f32[64,512]{1,0:T(8,128)S(1)}, u32[]{:S(2)}, u32[]{:S(2)}) %collective-permute-start.10) | collective-permute-done | bytes 131104 | tf_op jit(solution)/shard_map/ppermute | solution.py:202
  60.2 0.4 collective-permute-start.13
  60.6 0.1 collective-permute-start.12
  60.8 0.9 %collective-permute-done.13.refs_2_ = f32[64,512]{1,0:T(8,128)S(1)} collective-permute-done((f32[64,512]{1,0:T(8,128)S(1)}, f32[64,512]{1,0:T(8,128)S(1)}, u32[]{:S(2)}, u32[]{:S(2)}) %collective-permute-start.13) | collective-permute-done | bytes 131104 | tf_op jit(solution)/shard_map/ppermute | solution.py:210
  61.6 0.4 collective-permute-done.12.refs_1_
  62.0 1.6 %far_part.5 = f32[64,512]{1,0:T(8,128)} custom-call(bf16[512,2304]{1,0:T(8,128)(2,1)S(1)} %get-tuple-element.16.high_ref, bf16[512,2304]{1,0:T(8,128)(2,1)S(1)} %get-tuple-element.17.low_ref, f32[64,512]{1,0:T(8,128)S(1)} %chip_part.5.part_ref, f32[64,512]{1,0:T(8,128)S(1)} %collective-permute-done.9.refs_0_, f32[64,512]{1,0:T(8,128)S(1)} %collective-permute-done.12.refs_1_, ...), custom_call_target="tpu_custom_call" | custom-call | flops 226492416 | bytes 2359296 | tf_op jit(solution)/shard_map/far_part/pallas_call | solution.py:156
  (8 shorter events, 0.0 us)
Async XLA Ops:
  1.5 17.2 %all-to-all-start = ((f32[8,8,512]{2,0,1:T(8,128)}), f32[8,8,512]{2,0,1:T(8,128)S(1)}, u32[]{:S(2)}, u32[]{:S(2)}) async-start(f32[8,8,512]{2,0,1:T(8,128)} %bitcast.5), calls=%async_computation | async-start | bytes 262144 | tf_op jit(solution)/shard_map/all_to_all | solution.py:196
  9.8 12.1 %collective-permute-start.2 = (f32[64,512]{1,0:T(8,128)}, f32[64,512]{1,0:T(8,128)S(1)}, u32[]{:S(2)}, u32[]{:S(2)}) collective-permute-start(f32[64,512]{1,0:T(8,128)} %seeds_ref.5), channel_id=1, source_target_pairs={{0,1},{1,0},{2,3},{3,2},{4,5},{5,4},{6,7},{7,6},{8,9},{9,8},{10,11... | collective-permute-start | bytes 393224 | tf_op jit(solution)/shard_map/ppermute | solution.py:200
  9.8 12.9 %collective-permute-start.1 = (f32[64,512]{1,0:T(8,128)}, f32[64,512]{1,0:T(8,128)S(1)}, u32[]{:S(2)}, u32[]{:S(2)}) collective-permute-start(f32[64,512]{1,0:T(8,128)} %seeds_ref.5), channel_id=1, source_target_pairs={{0,2},{2,4},{3,1},{4,6},{5,3},{6,8},{7,5},{8,10},{9,7},{10,12},{11... | collective-permute-start | bytes 393224 | tf_op jit(solution)/shard_map/ppermute | solution.py:202
  18.7 7.0 %collective-permute-start = (f32[64,512]{1,0:T(8,128)}, f32[64,512]{1,0:T(8,128)S(1)}, u32[]{:S(2)}, u32[]{:S(2)}) collective-permute-start(f32[64,512]{1,0:T(8,128)} %seeds_ref.5), channel_id=1, source_target_pairs={{0,255},{1,2},{2,1},{3,4},{4,3},{5,6},{6,5},{7,8},{8,7},{9,10},{10... | collective-permute-start | bytes 393224 | tf_op jit(solution)/shard_map/ppermute | solution.py:201
  18.7 3.1 %copy-start = (f32[64,512]{1,0:T(8,128)S(1)}, f32[64,512]{1,0:T(8,128)}, u32[]{:S(2)}) copy-start(f32[64,512]{1,0:T(8,128)} %seeds_ref.5) | copy-start | bytes 393220
  25.7 1.3 %collective-permute-start.3 = (f32[64,512]{1,0:T(8,128)S(1)}, f32[64,512]{1,0:T(8,128)S(1)}, u32[]{:S(2)}, u32[]{:S(2)}) collective-permute-start(f32[64,512]{1,0:T(8,128)S(1)} %collective-permute-done.refs_1_), channel_id=1, source_target_pairs={{0,1},{1,0},{2,3},{3,2},{4,5},{5,4},{6,7},{7,6},{8,9},{9,8},{10,11... | collective-permute-start | bytes 393224 | tf_op jit(solution)/shard_map/ppermute | solution.py:206
  28.1 7.5 %collective-permute-start.6 = (f32[64,512]{1,0:T(8,128)S(1)}, f32[64,512]{1,0:T(8,128)S(1)}, u32[]{:S(2)}, u32[]{:S(2)}) collective-permute-start(f32[64,512]{1,0:T(8,128)S(1)} %far_part.3.own_ref), channel_id=1, source_target_pairs={{0,1},{1,0},{2,3},{3,2},{4,5},{5,4},{6,7},{7,6},{8,9},{9,8},{10,11... | collective-permute-start | bytes 393224 | tf_op jit(solution)/shard_map/ppermute | solution.py:200
  28.3 15.7 %collective-permute-start.5 = (f32[64,512]{1,0:T(8,128)S(1)}, f32[64,512]{1,0:T(8,128)S(1)}, u32[]{:S(2)}, u32[]{:S(2)}) collective-permute-start(f32[64,512]{1,0:T(8,128)S(1)} %far_part.3.own_ref), channel_id=1, source_target_pairs={{0,3},{1,254},{2,5},{3,0},{4,7},{5,2},{6,9},{7,4},{8,11},{9,6},{10... | collective-permute-start | bytes 393224 | tf_op jit(solution)/shard_map/ppermute | solution.py:202
  35.6 8.4 %collective-permute-start.4 = (f32[64,512]{1,0:T(8,128)S(1)}, f32[64,512]{1,0:T(8,128)S(1)}, u32[]{:S(2)}, u32[]{:S(2)}) collective-permute-start(f32[64,512]{1,0:T(8,128)S(1)} %far_part.3.own_ref), channel_id=1, source_target_pairs={{0,255},{1,2},{2,1},{3,4},{4,3},{5,6},{6,5},{7,8},{8,7},{9,10},{10... | collective-permute-start | bytes 393224 | tf_op jit(solution)/shard_map/ppermute | solution.py:201
  44.0 1.4 %collective-permute-start.8 = (f32[64,512]{1,0:T(8,128)S(1)}, f32[64,512]{1,0:T(8,128)S(1)}, u32[]{:S(2)}, u32[]{:S(2)}) collective-permute-start(f32[64,512]{1,0:T(8,128)S(1)} %collective-permute-done.5), channel_id=1, source_target_pairs={{0,1},{1,0},{2,3},{3,2},{4,5},{5,4},{6,7},{7,6},{8,9},{9,8},{10,11... | collective-permute-start | bytes 393224 | tf_op jit(solution)/shard_map/ppermute | solution.py:210
  44.4 1.3 %collective-permute-start.7 = (f32[64,512]{1,0:T(8,128)S(1)}, f32[64,512]{1,0:T(8,128)S(1)}, u32[]{:S(2)}, u32[]{:S(2)}) collective-permute-start(f32[64,512]{1,0:T(8,128)S(1)} %collective-permute-done.4.refs_0_), channel_id=1, source_target_pairs={{0,1},{1,0},{2,3},{3,2},{4,5},{5,4},{6,7},{7,6},{8,9},{9,8},{10,11... | collective-permute-start | bytes 393224 | tf_op jit(solution)/shard_map/ppermute | solution.py:210
  46.7 6.0 %collective-permute-start.11 = (f32[64,512]{1,0:T(8,128)S(1)}, f32[64,512]{1,0:T(8,128)S(1)}, u32[]{:S(2)}, u32[]{:S(2)}) collective-permute-start(f32[64,512]{1,0:T(8,128)S(1)} %far_part.4.own_ref), channel_id=1, source_target_pairs={{0,1},{1,0},{2,3},{3,2},{4,5},{5,4},{6,7},{7,6},{8,9},{9,8},{10,11... | collective-permute-start | bytes 393224 | tf_op jit(solution)/shard_map/ppermute | solution.py:200
  47.0 13.3 %collective-permute-start.10 = (f32[64,512]{1,0:T(8,128)S(1)}, f32[64,512]{1,0:T(8,128)S(1)}, u32[]{:S(2)}, u32[]{:S(2)}) collective-permute-start(f32[64,512]{1,0:T(8,128)S(1)} %far_part.4.own_ref), channel_id=1, source_target_pairs={{0,3},{1,254},{2,5},{3,0},{4,7},{5,2},{6,9},{7,4},{8,11},{9,6},{10... | collective-permute-start | bytes 393224 | tf_op jit(solution)/shard_map/ppermute | solution.py:202
  52.6 7.6 %collective-permute-start.9 = (f32[64,512]{1,0:T(8,128)S(1)}, f32[64,512]{1,0:T(8,128)S(1)}, u32[]{:S(2)}, u32[]{:S(2)}) collective-permute-start(f32[64,512]{1,0:T(8,128)S(1)} %far_part.4.own_ref), channel_id=1, source_target_pairs={{0,255},{1,2},{2,1},{3,4},{4,3},{5,6},{6,5},{7,8},{8,7},{9,10},{10... | collective-permute-start | bytes 393224 | tf_op jit(solution)/shard_map/ppermute | solution.py:201
  60.2 1.4 %collective-permute-start.13 = (f32[64,512]{1,0:T(8,128)S(1)}, f32[64,512]{1,0:T(8,128)S(1)}, u32[]{:S(2)}, u32[]{:S(2)}) collective-permute-start(f32[64,512]{1,0:T(8,128)S(1)} %collective-permute-done.10), channel_id=1, source_target_pairs={{0,1},{1,0},{2,3},{3,2},{4,5},{5,4},{6,7},{7,6},{8,9},{9,8},{10,11... | collective-permute-start | bytes 393224 | tf_op jit(solution)/shard_map/ppermute | solution.py:210
  60.6 1.3 %collective-permute-start.12 = (f32[64,512]{1,0:T(8,128)S(1)}, f32[64,512]{1,0:T(8,128)S(1)}, u32[]{:S(2)}, u32[]{:S(2)}) collective-permute-start(f32[64,512]{1,0:T(8,128)S(1)} %collective-permute-done.9.refs_0_), channel_id=1, source_target_pairs={{0,1},{1,0},{2,3},{3,2},{4,5},{5,4},{6,7},{7,6},{8,9},{9,8},{10,11... | collective-permute-start | bytes 393224 | tf_op jit(solution)/shard_map/ppermute | solution.py:210
